TPU v7x, 32 devices: a whole 2x2x4 slice. The times are simulated.
32 devices in a mesh: layer: 2 (over y), feat: 4 (over z), width: 4 (over x, core).
Axes of the slice: x: 2, y: 2, z: 4, core: 2. Of those that a mesh axis runs over, the one named last changes fastest.
Arguments:
- inputs: float32 [2, 1024, 2048], P('layer', None, 'width'), may hold values from -6 to 6
- targets: float32 [2, 1024, 2048], P(None, ('layer', 'feat'), 'width'), may hold values from -6 to 6
- w_enc: float32 [2, 2048, 16384], P('layer', 'width', 'feat'), may hold values from -0.125 to 0.125
- b_enc: float32 [2, 16384], P('layer', 'feat'), may hold values from -3 to 3
- thresholds: float32 [2, 16384], P('layer', 'feat'), may hold values from 0.2 to 1
- w_dec: float32 [2, 2, 16384, 2048], P('layer', None, 'feat', 'width'), may hold values from -0.046875 to 0.046875
- b_dec: float32 [2, 2048], P(None, 'width'), may hold values from -3 to 3
Outputs:
- dec_grad: float32 [2, 2, 16384, 2048], P('layer', None, 'feat', 'width')
- pre_grad: float32 [2, 1024, 16384], P('layer', 'width', 'feat')
All inputs are finite; a program needn't handle non-finite values.
Results may differ from a plain program's by a relative error of at most 0.0001.
Values sent between devices are 32-bit elements; how exact they have to be, the bound alone decides.
No kernel may reach another device: no remote copies, remote signals or barrier semaphores. Data moves between devices by JAX's collectives and lax.ppermute only.
A program may use at most 192 MiB of HBM per device.

v0:
```python
import jax
import jax.numpy as jnp
from jax import lax
from jax.sharding import PartitionSpec as P

softness = 0.5


def local(inputs, targets, w_enc, b_enc, thresholds, w_dec, b_dec):
    highest = lax.Precision.HIGHEST
    layer_pos = lax.axis_index("layer")
    layer_total = w_dec.shape[1]
    row_count = inputs.shape[1]
    partial_value = jnp.dot(
        inputs[0], w_enc[0], precision=highest, preferred_element_type=jnp.float32
    )
    pre_act = lax.psum(partial_value, "width") + b_enc[0][None, :]
    gate_open = jax.nn.sigmoid((pre_act - thresholds[0][None, :]) / softness)
    activations = pre_act * gate_open
    slope_val = gate_open + pre_act * gate_open * (1.0 - gate_open) / softness
    partials = []
    for target_pos in range(layer_total):
        product = jnp.dot(
            activations, w_dec[0, target_pos], precision=highest, preferred_element_type=jnp.float32
        )
        partials.append(jnp.where(target_pos >= layer_pos, product, 0.0))
    stacked = jnp.stack(partials)
    share_rows = targets.shape[1]
    row_start = lax.axis_index(("layer", "feat")) * share_rows
    own_rows = lax.dynamic_slice_in_dim(stacked, row_start, share_rows, 1) - targets
    stacked = lax.dynamic_update_slice(stacked, own_rows, (jnp.int32(0), row_start, jnp.int32(0)))
    errors = lax.psum(stacked, ("layer", "feat")) + b_dec[:, None, :]
    dec_grads = []
    for target_pos in range(layer_total):
        product = lax.dot_general(
            activations,
            errors[target_pos],
            (((0,), (0,)), ((), ())),
            precision=highest,
            preferred_element_type=jnp.float32,
        )
        dec_grads.append(jnp.where(target_pos >= layer_pos, product, 0.0))
    dec_grad = jnp.stack(dec_grads)[None]
    width_rows = row_count // lax.axis_size("width")
    back_sum = jnp.zeros((lax.axis_size("width") * width_rows, w_dec.shape[2]), jnp.float32)
    for target_pos in range(layer_total):
        product = lax.dot_general(
            errors[target_pos],
            w_dec[0, target_pos],
            (((1,), (1,)), ((), ())),
            precision=highest,
            preferred_element_type=jnp.float32,
        )
        back_sum = back_sum + jnp.where(target_pos >= layer_pos, product, 0.0)
    back_rows = lax.psum_scatter(back_sum, "width", scatter_dimension=0, tiled=True)
    slope_rows = lax.dynamic_slice_in_dim(
        slope_val, lax.axis_index("width") * width_rows, width_rows, 0
    )
    pre_grad = (back_rows * slope_rows)[None]
    return (dec_grad, pre_grad)


def solution(mesh):
    in_specs = (
        P("layer", None, "width"),
        P(None, ("layer", "feat"), "width"),
        P("layer", "width", "feat"),
        P("layer", "feat"),
        P("layer", "feat"),
        P("layer", None, "feat", "width"),
        P(None, "width"),
    )
    out_specs = (P("layer", None, "feat", "width"), P("layer", "width", "feat"))
    return jax.shard_map(local, mesh=mesh, in_specs=in_specs, out_specs=out_specs, check_vma=False)
```

profile of v0, /device:TPU:0, one launch (start us, length us, event | category | flops | bytes accessed | tf_op | source)
XLA Modules:
  0.0 770.8 jit_solution(10513116379828211835)
XLA Ops:
  7.2 0.0 copy-start
  7.2 0.0 all-reduce.3.cloned.1.call-start
  7.2 1.5 copy-done
  8.8 31.1 %fusion.8 = f32[1024,4096]{1,0:T(8,128)} fusion(f32[1,512,4096]{2,1,0:T(8,128)} %param.9, f32[1,1024,512]{2,1,0:T(8,128)S(1)} %copy-done), kind=kOutput, calls=%fused_computation.12 | convolution fusion | flops 25769803776 | bytes 27262976 | tf_op jit(solution)/shard_map/dot_general | solution.py:14
  39.9 0.0 copy-start.6
  39.9 0.0 copy-start.7
  39.9 0.0 all-reduce.3.cloned.1.call-update
  39.9 0.3 all-reduce.5.cloned.1.call-start
  40.2 290.9 %all-reduce.3.cloned.1.call-done = f32[1024,4096]{1,0:T(8,128)} async-done(((f32[1024,4096]{1,0:T(8,128)}), f32[1024,4096]{1,0:T(8,128)}) %all-reduce.3.cloned.1.call-update) | async-done | bytes 16777232 | tf_op jit(solution)/shard_map/psum | solution.py:17
  331.1 0.0 copy-done.6
  331.1 0.0 copy-done.7
  331.1 12.8 %add_divide_fusion = (f32[1024,4096]{1,0:T(8,128)}, f32[1024,4096]{1,0:T(8,128)S(1)}) fusion(f32[1024,4096]{1,0:T(8,128)} %all-reduce.3.cloned.1.call-done, f32[4096]{0:T(1024)S(1)} %bitcast.48, f32[4096]{0:T(1024)S(1)} %bitcast.49), kind=kLoop, calls=%fused_computation.2 | loop fusion | flops 29360128 | bytes 50364416 | tf_op jit(solution)/shard_map/div | solution.py:18
  343.9 0.0 copy-start.2
  343.9 30.1 %select_bitcast_fusion.2 = f32[1,1024,512]{2,1,0:T(8,128)S(1)} fusion(f32[1024,4096]{1,0:T(8,128)S(1)} %get-tuple-element.3, f32[1,2,4096,512]{3,2,1,0:T(8,128)} %param.12, pred[]{:T(512)S(6)} %le.5), kind=kOutput, calls=%fused_computation.32 | convolution fusion | flops 25770328064 | bytes 27262976 | tf_op jit(solution)/shard_map/dot_general | solution.py:23
  373.9 0.0 copy-done.2
  374.0 29.0 %select_bitcast_fusion.3 = f32[1,1024,512]{2,1,0:T(8,128)S(1)} fusion(f32[1024,4096]{1,0:T(8,128)S(1)} %get-tuple-element.3, f32[1,2,4096,512]{3,2,1,0:T(8,128)} %param.12, pred[]{:T(512)S(6)} %le.4), kind=kOutput, calls=%fused_computation.33 | convolution fusion | flops 25770328064 | bytes 27262976 | tf_op jit(solution)/shard_map/dot_general | solution.py:23
  402.9 0.0 copy-start.5
  402.9 0.0 copy-start.8
  402.9 2.5 pad_maximum_fusion
  405.5 0.0 copy-done.5
  405.5 0.9 fusion.27
  406.3 0.0 all-reduce.5.cloned.1.call-update
  406.4 0.0 reduce-scatter.2.cloned.1.call-start
  406.4 156.4 %all-reduce.5.cloned.1.call-done = f32[2,1024,512]{2,1,0:T(8,128)} async-done(((f32[2,1024,512]{2,1,0:T(8,128)}), f32[2,1024,512]{2,1,0:T(8,128)}) %all-reduce.5.cloned.1.call-update) | async-done | bytes 4194320 | tf_op jit(solution)/shard_map/psum | solution.py:32
  562.8 0.0 copy-done.8
  562.9 2.7 broadcast_add_fusion
  565.6 0.0 copy-start.3
  565.6 32.2 %fusion = f32[1024,4096]{1,0:T(8,128)S(1)} fusion(f32[1,2,4096,512]{3,2,1,0:T(8,128)} %param.12, f32[2,1024,512]{2,1,0:T(8,128)S(1)} %broadcast_add_fusion), kind=kOutput, calls=%fused_computation.4 | convolution fusion | flops 25769803776 | bytes 27262976 | tf_op jit(solution)/shard_map/dot_general | solution.py:47
  597.8 0.0 copy-done.3
  597.8 32.6 %select_add_fusion = f32[1024,4096]{1,0:T(8,128)} fusion(f32[1024,4096]{1,0:T(8,128)S(1)} %fusion, pred[]{:T(512)S(6)} %le.5, pred[]{:T(512)S(6)} %le.4, f32[1,2,4096,512]{3,2,1,0:T(8,128)} %param.12, f32[2,1024,512]{2,1,0:T(8,128)S(1)} %broadcast_add_fusion), kind=kOutput, calls=%fused_computation.1 | convolution fusion | flops 25782386688 | bytes 44040192 | tf_op jit(solution)/shard_map/dot_general | solution.py:47
  630.4 0.0 reduce-scatter.2.cloned.1.call-update
  630.4 0.0 copy-start.4
  630.4 30.8 %select_bitcast_fusion.1 = f32[1,4096,512]{2,1,0:T(8,128)S(1)} fusion(f32[1024,4096]{1,0:T(8,128)} %copy-done.2, pred[]{:T(512)S(6)} %le.4, f32[2,1024,512]{2,1,0:T(8,128)} %copy-done.3), kind=kOutput, calls=%fused_computation.15 | convolution fusion | flops 25771900928 | bytes 27262976 | tf_op jit(solution)/shard_map/dot_general | solution.py:35
  661.2 0.0 copy-done.4
  661.2 30.0 %select_bitcast_fusion = f32[1,4096,512]{2,1,0:T(8,128)S(1)} fusion(f32[1024,4096]{1,0:T(8,128)} %copy-done.2, pred[]{:T(512)S(6)} %le.5, f32[2,1024,512]{2,1,0:T(8,128)S(1)} %copy-done.4), kind=kOutput, calls=%fused_computation.14 | convolution fusion | flops 25771900928 | bytes 27262976 | tf_op jit(solution)/shard_map/dot_general | solution.py:35
  691.3 6.4 maximum_bitcast_fusion
  697.7 58.0 %reduce-scatter.2.cloned.1.call-done = f32[256,4096]{1,0:T(8,128)} async-done(((f32[1024,4096]{1,0:T(8,128)}), f32[256,4096]{1,0:T(8,128)}) %reduce-scatter.2.cloned.1.call-update) | async-done | bytes 4194320 | tf_op jit(solution)/shard_map/reduce_scatter | solution.py:55
  755.7 0.0 copy-start.1
  755.7 8.4 %fusion.19 = f32[1,256,4096]{2,1,0:T(8,128)} fusion(f32[256,4096]{1,0:T(8,128)} %reduce-scatter.2.cloned.1.call-done, f32[1024,4096]{1,0:T(8,128)} %copy-done.2, s32[]{:T(128)S(6)} %select_n.62, f32[1024,4096]{1,0:T(8,128)} %get-tuple-element.2), kind=kLoop, calls=%fused_computation.27 | loop fusion | flops 5242880 | bytes 16777220 | tf_op jit(solution)/shard_map/broadcast_in_dim | solution.py:59
  764.1 0.0 copy-done.1
Async XLA Ops:
  7.2 1.6 copy-start
  7.2 323.9 %all-reduce.3.cloned.1.call-start = ((), (), s32[]{:S(2)}) async-start(), calls=%async_computation.1 | async-start | bytes 33554432 | tf_op jit(solution)/shard_map/psum | solution.py:17
  39.9 291.2 %copy-start.6 = (f32[1,4096]{1,0:T(1,128)S(1)}, f32[1,4096]{1,0:T(1,128)}, u32[]{:S(2)}) copy-start(f32[1,4096]{1,0:T(1,128)} %param.11) | copy-start | bytes 49156
  39.9 291.2 %copy-start.7 = (f32[1,4096]{1,0:T(1,128)S(1)}, f32[1,4096]{1,0:T(1,128)}, u32[]{:S(2)}) copy-start(f32[1,4096]{1,0:T(1,128)} %param.10) | copy-start | bytes 49156
  39.9 522.9 %all-reduce.5.cloned.1.call-start = ((), (), s32[]{:S(2)}) async-start(), calls=%async_computation.2 | async-start | bytes 8388608 | tf_op jit(solution)/shard_map/psum | solution.py:32
  343.9 30.1 %copy-start.2 = (f32[1024,4096]{1,0:T(8,128)}, f32[1024,4096]{1,0:T(8,128)S(1)}, u32[]{:S(2)}) copy-start(f32[1024,4096]{1,0:T(8,128)S(1)} %get-tuple-element.3) | copy-start | bytes 50331652
  402.9 2.5 copy-start.5
  402.9 159.9 %copy-start.8 = (f32[2,512]{1,0:T(2,128)S(1)}, f32[2,512]{1,0:T(2,128)}, u32[]{:S(2)}) copy-start(f32[2,512]{1,0:T(2,128)} %param.13) | copy-start | bytes 12292
  406.4 349.3 %reduce-scatter.2.cloned.1.call-start = ((), (), s32[]{:S(2)}) async-start(), calls=%async_computation.3 | async-start | bytes 20971520 | tf_op jit(solution)/shard_map/reduce_scatter | solution.py:55
  565.6 32.2 %copy-start.3 = (f32[2,1024,512]{2,1,0:T(8,128)}, f32[2,1024,512]{2,1,0:T(8,128)S(1)}, u32[]{:S(2)}) copy-start(f32[2,1024,512]{2,1,0:T(8,128)S(1)} %broadcast_add_fusion) | copy-start | bytes 12582916
  630.4 30.8 %copy-start.4 = (f32[2,1024,512]{2,1,0:T(8,128)S(1)}, f32[2,1024,512]{2,1,0:T(8,128)}, u32[]{:S(2)}) copy-start(f32[2,1024,512]{2,1,0:T(8,128)} %copy-done.3) | copy-start | bytes 12582916
  755.7 8.4 %copy-start.1 = (f32[1,1024,512]{2,1,0:T(8,128)S(1)}, f32[1,1024,512]{2,1,0:T(8,128)}, u32[]{:S(2)}) copy-start(f32[1,1024,512]{2,1,0:T(8,128)} %param.7) | copy-start | bytes 6291460
Sparse Core Ops, SparseCore 0:
  40.0 290.9 all-reduce.2
  406.5 156.3 all-reduce.4
  630.5 125.1 reduce-scatter.1
where the time goes:
time: 776 us; the launch traced here: 771 us
  waiting for transfers between devices  505 us (65%)
  matrix products  216 us (28%)
  other arithmetic  33.7 us (4%)
  between operations  14.1 us (2%)
    psum x1, waiting for transfers between devices, local(): pre_act = lax.psum(partial_value, 'width') + b_enc[0][None, :]  291 us
    psum x1, waiting for transfers between devices, local(): errors = lax.psum(stacked, ('layer', 'feat')) + b_dec[:, None, :]  156 us
    dot_general x2, matrix products, local(): lax.dot_general(errors[target_pos], w_dec[0, target_pos], (((1,), (1,)),...  64.8 us
    dot_general x2, matrix products, local(): lax.dot_general(activations, errors[target_pos], (((0,), (0,)), ((), ()))...  60.9 us
    dot_general x2, matrix products, local(): jnp.dot(activations, w_dec[0, target_pos], precision=highest, preferred_e...  59 us
    reduce_scatter x1, waiting for transfers between devices, local(): lax.psum_scatter(back_sum, 'width', scatter_dimension=0, tiled=True)  58 us
    dot_general x1, matrix products, local(): jnp.dot(inputs[0], w_enc[0], precision=highest, preferred_element_type=jn...  31.1 us
  transfers between devices with their start and end apart: 3, of which 3 were waited for; matrix products, arithmetic and copies ran while one was open for 9% of the time, Pallas kernels for 0%

commit v1 on v0

v1 whole, which is shorter than its diff:
```python
import functools

import jax
import jax.numpy as jnp
from jax import lax
from jax.experimental import pallas as pl
from jax.experimental.pallas import tpu as pltpu
from jax.sharding import PartitionSpec as P

softness = 0.5
eighths = (1, 1, 2, 2, 1, 1)
cuts = 4
f32 = jnp.float32
bf16 = jnp.bfloat16
anywhere = pl.BlockSpec(memory_space=pl.ANY)
scalars = pl.BlockSpec(memory_space=pltpu.SMEM)
vector = pl.BlockSpec(memory_space=pltpu.VMEM)
hbm = pl.BlockSpec(memory_space=pltpu.HBM)
granted = 46 * 1024 * 1024


def pieces_of(rows):
    if rows % 128:
        return [(0, rows)]
    bounds = [0]
    for part in eighths:
        bounds.append(bounds[-1] + part * rows // 8)
    return list(zip(bounds[:-1], bounds[1:]))


def halves(value):
    high = value.astype(bf16)
    return high, (value - high.astype(f32)).astype(bf16)


def three(a_high, a_low, b_high, b_low, dims):
    dot = functools.partial(
        lax.dot_general, dimension_numbers=(dims, ((), ())), preferred_element_type=f32
    )
    return dot(a_high, b_high) + (dot(a_low, b_high) + dot(a_high, b_low))


plain = ((1,), (0,))
across_rows = ((0,), (0,))
across_columns = ((1,), (1,))


def shape(dims, kind=f32):
    return jax.ShapeDtypeStruct(dims, kind)


def loop(total, step, body):
    def turn(k, carry):
        body(pl.ds(pl.multiple_of(k * step, step), step))
        return carry

    lax.fori_loop(0, total // step, turn, 0)


def join(refs, columns):
    return jnp.concatenate([r[:, columns] for r in refs])


class Chain:
    def __init__(self):
        self.last = None

    def __call__(
        self, name, body, inputs, outputs, scratch=(), aliases=None, grid=None
    ):
        arrays = [a for a, _ in inputs]
        in_specs = [s for _, s in inputs]
        extra = 0
        if self.last is not None:
            arrays.append(self.last)
            in_specs.append(anywhere)
            extra = 1
        count = len(inputs)
        given = len(outputs)

        def kernel(*refs):
            ins = refs[:count]
            outs = refs[count + extra : count + extra + given]
            mark = refs[count + extra + given]
            mark[...] = jnp.zeros_like(mark)
            body(ins, outs, *refs[count + extra + given + 1 :])

        mark_spec = vector if grid is None else pl.BlockSpec((8, 128), lambda *i: (0, 0))
        result = pl.pallas_call(
            kernel,
            grid=grid or (),
            in_specs=in_specs,
            out_specs=[s for _, s in outputs] + [mark_spec],
            out_shape=[o for o, _ in outputs] + [shape((8, 128))],
            scratch_shapes=list(scratch),
            input_output_aliases=aliases or {},
            compiler_params=pltpu.CompilerParams(vmem_limit_bytes=granted),
            cost_estimate=pl.CostEstimate(flops=0, bytes_accessed=0, transcendentals=0),
            name=name,
        )(*arrays)
        self.last = result[-1]
        return result[:-1]


def stream(count, copy, body):
    copy(0).start()
    for k in range(count):
        if k + 1 < count:
            copy(k + 1).start()
        copy(k).wait()
        body(k, k % 2)


def local(inputs, targets, w_enc, b_enc, thresholds, w_dec, b_dec):
    layer_pos = lax.axis_index("layer")
    first = layer_pos == 0
    feat_pos = lax.axis_index("feat")
    feat_size = lax.axis_size("feat")
    width = lax.axis_size("width")
    pos = lax.axis_index("width")
    near = pos % 2
    far = pos // 2
    tokens = inputs.shape[1]
    model = inputs.shape[2]
    feats = w_enc.shape[2]
    share = tokens // width
    tile = min(512, feats)
    wide = min(1024, feats)
    wides = feats // wide
    group = min(model, wide)
    groups = wide // group
    shared = (groups * model, group) == (wide, model)
    blocks = 3 * wides if shared else wides
    skipped = wides if shared else 0
    near_pairs = [(i, i ^ 1) for i in range(width)]
    far_pairs = [(i, i ^ 2) for i in range(width)]
    pieces = pieces_of(share)
    flags = jnp.stack([first.astype(jnp.int32), far.astype(jnp.int32)])

    def swap_near(arrays):
        return [lax.ppermute(a, "width", near_pairs) for a in arrays]

    def swap_far(a):
        return lax.ppermute(a, "width", far_pairs)

    def arrange(rows):
        split = rows.reshape(2, 2, share, rows.shape[-1])
        found = []
        for lo, hi in pieces:
            cut = split[:, :, lo:hi]
            own = lax.dynamic_index_in_dim(cut, near, 1, keepdims=False)
            other = lax.dynamic_index_in_dim(cut, 1 - near, 1, keepdims=False)
            found.append(jnp.stack([own, other]).reshape(-1, model))
        return found

    x_rows = arrange(inputs[0])
    chain = Chain()
    store = [{} for _ in pieces]
    weights = {}
    saved = {}

    def size(i):
        return pieces[i][1] - pieces[i][0]

    def cut_rows(i):
        return 2 * size(i) // cuts

    def cut_shapes(i):
        return [(shape((cut_rows(i), feats)), vector)] * cuts

    def write_cuts(i, value, own, others, columns):
        n = size(i)
        own[:, columns] = value[: 2 * n]
        for k, out in enumerate(others):
            start = 2 * n + k * cut_rows(i)
            out[:, columns] = value[start : start + cut_rows(i)]

    def fetch(source, buffers, sems):
        return lambda k: pltpu.make_async_copy(source.at[k], buffers.at[k % 2], sems.at[k % 2])

    def fetch_pairs(source, buffers, sems):
        return lambda k: pltpu.make_async_copy(
            source.at[pl.ds(skipped + 2 * k, 2)], buffers.at[k % 2], sems.at[k % 2]
        )

    def enter(i):
        n = size(i)

        def body(ins, outs, buffers, made, sems):
            x, w = ins
            own, *others, kept = outs
            x_high, x_low = halves(x[...])

            def read(k):
                return pltpu.make_async_copy(
                    w.at[0, :, pl.ds(k * wide, wide)], buffers.at[k % 2], sems.at[k % 2]
                )

            def write(k):
                return pltpu.make_async_copy(made.at[k % 2], kept.at[k], sems.at[2 + k % 2])

            def step(k, slot):
                w_high, w_low = halves(buffers[slot])
                if k >= 2:
                    write(k - 2).wait()
                for g in range(groups):
                    rows, cut = slice(g * model, (g + 1) * model), slice(g * group, (g + 1) * group)
                    made[slot, 0, rows], made[slot, 1, rows] = w_high[:, cut], w_low[:, cut]
                write(k).start()
                columns = slice(k * wide, (k + 1) * wide)
                write_cuts(i, three(x_high, x_low, w_high, w_low, plain), own, others, columns)

            stream(wides, read, step)
            for k in range(max(wides - 2, 0), wides):
                write(k).wait()

        own, *others, weights["enc"] = chain(
            "enter",
            body,
            [(x_rows[i], vector), (w_enc, hbm)],
            [(shape((2 * n, feats)), vector)]
            + cut_shapes(i)
            + [(shape((blocks, 2, groups * model, group), bf16), hbm)],
            scratch=[
                pltpu.VMEM((2, model, wide), f32),
                pltpu.VMEM((2, 2, groups * model, group), bf16),
                pltpu.SemaphoreType.DMA((4,)),
            ],
        )
        store[i]["own"], store[i]["in"] = own, swap_near(others)

    def part(i):
        n = size(i)

        def body(ins, outs, buffers, sems):
            x, w = ins
            own, *others = outs

            def step(k, slot):
                x_high, x_low = halves(x[...])
                for g in range(groups):
                    rows = slice(g * model, (g + 1) * model)
                    value = three(x_high, x_low, buffers[slot, 0, rows], buffers[slot, 1, rows], plain)
                    start = k * wide + g * group
                    write_cuts(i, value, own, others, slice(start, start + group))

            stream(wides, fetch(w, buffers, sems), step)

        own, *others = chain(
            "part",
            body,
            [(x_rows[i], vector), (weights["enc"], hbm)],
            [(shape((2 * n, feats)), vector)] + cut_shapes(i),
            scratch=[
                pltpu.VMEM((2, 2, groups * model, group), bf16),
                pltpu.SemaphoreType.DMA((2,)),
            ],
        )
        store[i]["own"], store[i]["in"] = own, swap_near(others)

    def summed(i):
        n = size(i)

        def body(ins, outs):
            own, *others = ins

            def step(columns):
                outs[0][:, columns] = own[:, columns] + join(others, columns)

            loop(feats, wide, step)

        (value,) = chain(
            "chip_sum",
            body,
            [(a, vector) for a in [store[i]["own"], *store[i]["in"]]],
            [(shape((2 * n, feats)), vector)],
        )
        store[i]["sum"], store[i]["in"] = value, swap_far(value)

    def split_decoder():
        def body(ins, outs, buffers, made, sems):
            w, kept = ins[0], outs[0]

            def read(k):
                return pltpu.make_async_copy(
                    w.at[0, :, pl.ds(k * wide, wide)], buffers.at[k % 2], sems.at[k % 2]
                )

            def write(k):
                return pltpu.make_async_copy(
                    made.at[k % 2], kept.at[pl.ds(skipped + 2 * k, 2)], sems.at[2 + k % 2]
                )

            def step(k, slot):
                if k >= 2:
                    write(k - 2).wait()
                for t in range(2):
                    made[slot, t, 0], made[slot, t, 1] = halves(buffers[slot, t])
                write(k).start()

            stream(wides, read, step)
            for k in range(max(wides - 2, 0), wides):
                write(k).wait()

        (weights["dec"],) = chain(
            "split_decoder",
            body,
            [(w_dec, hbm)] + ([(weights["enc"], hbm)] if shared else []),
            [(shape((skipped + 2 * wides, 2, wide, model), bf16), hbm)],
            aliases={1: 0} if shared else {},
            scratch=[
                pltpu.VMEM((2, 2, wide, model), f32),
                pltpu.VMEM((2, 2, 2, wide, model), bf16),
                pltpu.SemaphoreType.DMA((4,)),
            ],
        )
        if shared:
            weights["enc"] = weights["dec"]

    def goals():
        share_rows = targets.shape[1]

        def body(ins, outs):
            flag, goal = ins
            home, away = outs
            own = flag[0] == 1
            home[...] = jnp.where(own, goal[0], goal[1])
            away[...] = jnp.where(own, goal[1], goal[0])

        home, away = chain(
            "targets",
            body,
            [(flags, scalars), (targets, vector)],
            [(shape((share_rows, model)), vector)] * 2,
        )
        away = lax.ppermute(away, "layer", [(0, 1), (1, 0)])
        padded = jnp.zeros((tokens, model), f32)
        home_start = (layer_pos * feat_size + feat_pos) * share_rows
        away_start = ((1 - layer_pos) * feat_size + feat_pos) * share_rows
        padded = lax.dynamic_update_slice(padded, home, (home_start, jnp.int32(0)))
        padded = lax.dynamic_update_slice(padded, away, (away_start, jnp.int32(0)))
        weights["goal"] = arrange(padded)

    def gate(i):
        n = size(i)

        def body(ins, outs):
            flag, s, r, b, th = ins
            *acts, slope = outs

            def step(columns):
                bias, edge = b[:, columns], th[:, columns]

                def opened(pre):
                    return jax.nn.sigmoid((pre - edge) / softness)

                for k, out in enumerate(acts):
                    rows = slice(k * cut_rows(i), (k + 1) * cut_rows(i))
                    pre = s[rows, columns] + r[rows, columns] + bias
                    out[:, columns] = pre * opened(pre)
                rows = pl.ds(pl.multiple_of(flag[1] * n, n), n)
                pre = s[rows, columns] + r[rows, columns] + bias
                own = opened(pre)
                slope[:, columns] = own + pre * own * (1.0 - own) / softness

            loop(feats, wide, step)

        *acts, slope = chain(
            "gate",
            body,
            [
                (flags, scalars),
                (store[i]["sum"], vector),
                (store[i]["in"], vector),
                (b_enc, vector),
                (thresholds, vector),
            ],
            cut_shapes(i) + [(shape((n, feats)), vector)],
        )
        store[i]["acts"], store[i]["slope"], store[i]["in"] = acts, slope, swap_near(acts)

    def keep(name, ins, outs, columns):
        aliases = {}
        if name in saved:
            aliases = {len(ins): len(outs)}
            ins.append((saved[name], hbm))
        outs.append((shape((2, tokens, columns), bf16), hbm))
        return aliases

    def recon(i):
        n = size(i)
        lo = pieces[i][0]

        def body(ins, outs, buffers, made, sems):
            own, other, w = ins[:cuts], ins[cuts : 2 * cuts], ins[2 * cuts]
            r0, r1, kept = outs

            def save(k):
                rows, columns = pl.ds(4 * lo, 4 * n), pl.ds(k * wide, wide)
                return pltpu.make_async_copy(
                    made.at[k % 2], kept.at[:, rows, columns], sems.at[2 + k % 2]
                )

            def step(k, slot):
                columns = slice(k * wide, (k + 1) * wide)
                a_high, a_low = halves(join(own + other, columns))
                if k >= 2:
                    save(k - 2).wait()
                made[slot, 0], made[slot, 1] = a_high, a_low
                save(k).start()
                for t, out in enumerate((r0, r1)):
                    value = three(a_high, a_low, buffers[slot, t, 0], buffers[slot, t, 1], plain)
                    out[...] = out[...] + value if k else value

            stream(wides, fetch_pairs(w, buffers, sems), step)
            for k in range(max(wides - 2, 0), wides):
                save(k).wait()

        ins = [(a, vector) for a in [*store[i]["acts"], *store[i]["in"]]] + [(weights["dec"], hbm)]
        outs = [(shape((4 * n, model)), vector)] * 2
        aliases = keep("acts", ins, outs, feats)
        r0, r1, saved["acts"] = chain(
            "recon",
            body,
            ins,
            outs,
            scratch=[pltpu.VMEM((2, 2, 2, wide, model), bf16)]
            + [pltpu.VMEM((2, 2, 4 * n, wide), bf16)]
            + [pltpu.SemaphoreType.DMA((4,))],
            aliases=aliases,
        )
        store[i]["r"] = (r0, r1)
        store[i]["in"] = lax.ppermute(r1, "layer", [(0, 1)])

    def held(i):
        n = size(i)

        def body(ins, outs):
            flag, r0, r1, below, goal = ins
            outs[0][...] = jnp.where(flag[0] == 1, r0[...], r1[...] + below[...]) - goal[...]

        arrays = [*store[i]["r"], store[i]["in"], weights["goal"][i]]
        (value,) = chain(
            "held",
            body,
            [(flags, scalars)] + [(a, vector) for a in arrays],
            [(shape((4 * n, model)), vector)],
        )
        store[i]["held"] = value
        if feat_size <= 4:
            store[i]["in"] = lax.ppermute(value, "feat", [(k, k ^ 1) for k in range(feat_size)])
        else:
            store[i]["in"] = lax.psum(value, "feat")
            store[i]["held"] = jnp.zeros_like(value)

    def middle(i):
        n = size(i)
        if feat_size > 4:
            return

        def body(ins, outs):
            outs[0][...] = ins[0][...] + ins[1][...]

        (value,) = chain(
            "feat_sum",
            body,
            [(store[i]["held"], vector), (store[i]["in"], vector)],
            [(shape((4 * n, model)), vector)],
        )
        store[i]["held"] = value
        store[i]["in"] = lax.ppermute(value, "feat", [(k, k ^ 2) for k in range(feat_size)])

    def across(i):
        n = size(i)

        def body(ins, outs):
            flag, a, b, bias = ins
            line = jnp.where(flag[0] == 1, bias[0:1, :], bias[1:2, :])
            outs[0][...] = a[...] + b[...] + line

        (value,) = chain(
            "errors",
            body,
            [(flags, scalars)] + [(a, vector) for a in (store[i]["held"], store[i]["in"], b_dec)],
            [(shape((4 * n, model)), vector)],
        )
        store[i]["held"] = value
        store[i]["in"] = lax.ppermute(value, "layer", [(1, 0)])

    def back(i):
        n = size(i)
        lo = pieces[i][0]

        def body(ins, outs, buffers, made, sems):
            flag, value, above, w = ins[:4]
            own, *others, kept = outs
            e_high, e_low = made.at[0], made.at[1]
            is_first = flag[0] == 1
            zero = jnp.where(is_first, value[...], 0.0)
            one = jnp.where(is_first, above[...], value[...])
            e_high[:, :model], e_low[:, :model] = halves(zero)
            e_high[:, model:], e_low[:, model:] = halves(one)
            copy = pltpu.make_async_copy(made, kept.at[:, pl.ds(4 * lo, 4 * n)], sems.at[2])
            copy.start()

            def step(k, slot):
                total = None
                for t in range(2):
                    cut = slice(t * model, (t + 1) * model)
                    high, low = buffers[slot, t, 0], buffers[slot, t, 1]
                    term = three(e_high[:, cut], e_low[:, cut], high, low, across_columns)
                    total = term if total is None else total + term
                write_cuts(i, total, own, others, slice(k * wide, (k + 1) * wide))

            stream(wides, fetch_pairs(w, buffers, sems), step)
            copy.wait()

        arrays = [store[i]["held"], store[i]["in"]]
        ins = [(flags, scalars)] + [(a, vector) for a in arrays] + [(weights["dec"], hbm)]
        outs = [(shape((2 * n, feats)), vector)] + cut_shapes(i)
        aliases = keep("errors", ins, outs, 2 * model)
        own, *others, saved["errors"] = chain(
            "back",
            body,
            ins,
            outs,
            scratch=[pltpu.VMEM((2, 2, 2, wide, model), bf16)]
            + [pltpu.VMEM((2, 4 * n, 2 * model), bf16)]
            + [pltpu.SemaphoreType.DMA((3,))],
            aliases=aliases,
        )
        store[i]["own"], store[i]["in"] = own, swap_near(others)

    def turn(i):
        n = size(i)
        half = cuts // 2

        def body(ins, outs):
            flag, own, *others = ins
            mine, theirs = outs
            for place in range(2):

                @pl.when(flag[1] == place)
                def _():
                    for out, at in ((mine, place), (theirs, 1 - place)):

                        def step(columns):
                            arrived = join(others[at * half : (at + 1) * half], columns)
                            out[:, columns] = own[at * n : (at + 1) * n, columns] + arrived

                        loop(feats, wide, step)

        mine, theirs = chain(
            "turn",
            body,
            [(flags, scalars)] + [(a, vector) for a in [store[i]["own"], *store[i]["in"]]],
            [(shape((n, feats)), vector)] * 2,
        )
        store[i]["own"], store[i]["in"] = mine, swap_far(theirs)

    def finish(i):
        lo, hi = pieces[i]
        n = size(i)

        def body(ins, outs, value, sem):
            mine, arrived, slope = ins[:3]

            def step(columns):
                value[:, columns] = (mine[:, columns] + arrived[:, columns]) * slope[:, columns]

            loop(feats, wide, step)
            copy = pltpu.make_async_copy(value, outs[0].at[0, pl.ds(lo, n)], sem)
            copy.start()
            copy.wait()

        ins = [(store[i][k], vector) for k in ("own", "in", "slope")]
        aliases = {}
        if "grad" in saved:
            aliases = {len(ins): 0}
            ins.append((saved["grad"], hbm))
        (saved["grad"],) = chain(
            "finish",
            body,
            ins,
            [(shape((1, share, feats)), hbm)],
            scratch=[pltpu.VMEM((n, feats), f32), pltpu.SemaphoreType.DMA],
            aliases=aliases,
        )

    def decoder_grad():
        def body(ins, outs):
            a, e = ins
            value = three(a[0], a[1], e[0], e[1], across_rows)
            outs[0][0, 0] = value[:, :model]
            outs[0][0, 1] = value[:, model:]

        (out,) = chain(
            "decoder_grad",
            body,
            [
                (saved["acts"], pl.BlockSpec((2, tokens, tile), lambda j: (0, 0, j))),
                (saved["errors"], pl.BlockSpec((2, tokens, 2 * model), lambda j: (0, 0, 0))),
            ],
            [(shape((1, 2, feats, model)), pl.BlockSpec((1, 2, tile, model), lambda j: (0, 0, j, 0)))],
            grid=(feats // tile,),
        )
        return out

    last = len(pieces)

    def at(f, i):
        if 0 <= i < last:
            f(i)

    enter(0)
    summed(0)
    split_decoder()
    at(part, 1)
    goals()
    at(summed, 1)
    for i in range(last + 1):
        at(gate, i)
        at(part, i + 2)
        at(recon, i)
        at(across, i - 1)
        at(summed, i + 2)
        if i == last - 1:
            at(finish, 0)
        at(held, i)
        at(back, i - 1)
        at(middle, i)
        at(turn, i - 1)
        if i == last - 1:
            at(finish, 1)
    dec_grad = decoder_grad()
    for i in range(2, last):
        finish(i)
    return dec_grad, saved["grad"]


def solution(mesh):
    in_specs = (
        P("layer", None, "width"),
        P(None, ("layer", "feat"), "width"),
        P("layer", "width", "feat"),
        P("layer", "feat"),
        P("layer", "feat"),
        P("layer", None, "feat", "width"),
        P(None, "width"),
    )
    out_specs = (P("layer", None, "feat", "width"), P("layer", "width", "feat"))
    return jax.shard_map(local, mesh=mesh, in_specs=in_specs, out_specs=out_specs, check_vma=False)
```

time: 776 us -> 471 us (0.61)
  waiting for transfers between devices: 505 us -> 142 us
  Pallas kernels: 0 us -> 234 us
  matrix products: 216 us -> 0 us
  starting transfers between devices: 0.33 us -> 71.8 us
  other arithmetic: 33.7 us -> 0.37 us
  local copies, waits for them, and re-layouts: 1.59 us -> 16.7 us
  between operations: 14.1 us -> 2.27 us
    psum x2 -> x0, waiting for transfers between devices: 447 us -> none  [the longest x1 291 us: local(): pre_act = lax.psum(partial_value, 'width') + b_enc[0][None, :]]
    pallas_call x0 -> x63, Pallas kernels: none -> 234 us  [__call__(): pl.pallas_call(kernel, grid=grid or (), in_specs=in_specs, out_specs=[s f...]
    dot_general x7 -> x0, matrix products: 216 us -> none  [the longest x2 64.8 us: local(): lax.dot_general(errors[target_pos], w_dec[0, target_pos], (((1,), (1,)),...]
    ppermute x0 -> x109, waiting for transfers between devices: none -> 142 us  [the longest x6 41.6 us: middle(): lax.ppermute(value, 'feat', [(k, k ^ 2) for k in range(feat_size)])]
    ppermute x0 -> x109, starting transfers between devices: none -> 71.8 us  [the longest x6 18.6 us: recon(): store[i]['in'] = lax.ppermute(r1, 'layer', [(0, 1)])]
    reduce_scatter x1 -> x0, waiting for transfers between devices: 58 us -> none  [local(): lax.psum_scatter(back_sum, 'width', scatter_dimension=0, tiled=True)]
    broadcast_in_dim x2 -> x0, other arithmetic: 14.8 us -> none  [the longest x1 8.38 us: local(): pre_grad = (back_rows * slope_rows)[None]]
    div x1 -> x0, other arithmetic: 12.8 us -> none  [local(): gate_open = jax.nn.sigmoid((pre_act - thresholds[0][None, :]) / softness)]
  transfers between devices with their start and end apart: 3 -> 109, of which waited for: 3 -> 55; matrix products, arithmetic and copies ran while one was open for 9% -> 1% of each run, Pallas kernels for 0% -> 47%
where the time goes in v1:
time: 471 us; the launch traced here: 467 us
  Pallas kernels  234 us (50%)
  waiting for transfers between devices  142 us (30%)
  starting transfers between devices  71.8 us (15%)
  local copies, waits for them, and re-layouts  16.7 us (4%)
    pallas_call x63, Pallas kernels, __call__(): pl.pallas_call(kernel, grid=grid or (), in_specs=in_specs, out_specs=[s f...  234 us
    ppermute x6, waiting for transfers between devices, middle(): lax.ppermute(value, 'feat', [(k, k ^ 2) for k in range(feat_size)])  41.6 us
    ppermute x6, waiting for transfers between devices, across(): store[i]['in'] = lax.ppermute(value, 'layer', [(1, 0)])  38.7 us
    ppermute x6, waiting for transfers between devices, recon(): store[i]['in'] = lax.ppermute(r1, 'layer', [(0, 1)])  20.1 us
    ppermute x6, starting transfers between devices, recon(): store[i]['in'] = lax.ppermute(r1, 'layer', [(0, 1)])  18.6 us
    ppermute x72, starting transfers between devices, swap_near(): return [lax.ppermute(a, 'width', near_pairs) for a in arrays]  17.5 us
    ppermute x72, waiting for transfers between devices, swap_near(): return [lax.ppermute(a, 'width', near_pairs) for a in arrays]  17.1 us
    ppermute x12, starting transfers between devices, swap_far(): return lax.ppermute(a, 'width', far_pairs)  14.5 us
  transfers between devices with their start and end apart: 109, of which 55 were waited for; matrix products, arithmetic and copies ran while one was open for 1% of the time, Pallas kernels for 47%

profile of v1, /device:TPU:0, one launch (start us, length us, event | category | flops | bytes accessed | tf_op | source)
XLA Modules:
  0.0 466.7 jit_solution(8986289095858392039)
XLA Ops:
  2.7 8.7 %enter.1 = (f32[64,4096]{1,0:T(8,128)S(1)}, f32[16,4096]{1,0:T(8,128)S(1)}, f32[16,4096]{1,0:T(8,128)S(1)}, f32[16,4096]{1,0:T(8,128)S(1)}, f32[16,4096]{1,0:T(8...) custom-call(f32[128,512]{1,0:T(8,128)S(1)} %bitcast.71, f32[1,512,4096]{2,1,0:T(8,128)} %refs_1_.2), custom_call_target="tpu_custom_call" | custom-call | tf_op jit(solution)/shard_map/enter/pallas_call | solution.py:89
  14.7 2.9 collective-permute-start.9
  18.5 11.9 %split_decoder.1 = (bf16[12,2,1024,512]{3,2,1,0:T(8,128)(2,1)}, f32[8,128]{1,0:T(8,128)S(1)}) custom-call(f32[1,2,4096,512]{3,2,1,0:T(8,128)} %refs_0_.1, bf16[12,2,1024,512]{3,2,1,0:T(8,128)(2,1)} %get-tuple-element.225.refs_1_, f32[8,128]{1,0:T(8,128)S(1)} %get-tuple-element.232.refs_2_), custom_call_target="tpu_custom_call", output_to_operand_aliasing={{0}: (1, {})} | custom-call | tf_op jit(solution)/shard_map/split_decoder/pallas_call | solution.py:89
  30.4 5.1 %part.5 = (f32[64,4096]{1,0:T(8,128)S(1)}, f32[16,4096]{1,0:T(8,128)S(1)}, f32[16,4096]{1,0:T(8,128)S(1)}, f32[16,4096]{1,0:T(8,128)S(1)}, f32[16,4096]{1,0:T(8,128)S(1)}, /*index=5*/f32[8,128]{1,0:T(8,128)S(1)}) custom-call(f32[128,512]{1,0:T(8,128)S(1)} %bitcast.68, bf16[12,2,1024,512]{3,2,1,0:T(8,128)(2,1)} %get-tuple-element.233.refs_1_.refs_8_.refs_3_, ...), custom_call_target="tpu_custom_call" | custom-call | tf_op jit(solution)/shard_map/part/pallas_call | solution.py:89
  44.2 7.4 %part.6 = (f32[128,4096]{1,0:T(8,128)S(1)}, f32[32,4096]{1,0:T(8,128)}, f32[32,4096]{1,0:T(8,128)}, f32[32,4096]{1,0:T(8,128)}, f32[32,4096]{1,0:T(8,128)}, /*index=5*/f32[8,128]{1,0:T(8,128)S(1)}) custom-call(f32[256,512]{1,0:T(8,128)S(1)} %bitcast.67, bf16[12,2,1024,512]{3,2,1,0:T(8,128)(2,1)} %get-tuple-element.233.refs_1_.refs_8_.refs_3_, ...), custom_call_target="tpu_custom_call" | custom-call | tf_op jit(solution)/shard_map/part/pallas_call | solution.py:89
  64.7 8.2 %recon.6 = (f32[128,512]{1,0:T(8,128)S(1)}, f32[128,512]{1,0:T(8,128)S(1)}, bf16[2,1024,4096]{2,1,0:T(8,128)(2,1)}, f32[8,128]{1,0:T(8,128)S(1)}) custom-call(f32[16,4096]{1,0:T(8,128)S(1)} %get-tuple-element.245.refs_0_, f32[16,4096]{1,0:T(8,128)S(1)} %copy-done.14, f32[16,4096]{1,0:T(8,128)S(1)} %copy-done.16, f32[16,4096]{1,0:T(8,128)S(1)} %copy-done.18, ...), custom_call_target="tpu_custom_call" | custom-call | tf_op jit(solution)/shard_map/recon/pallas_call | solution.py:89
  72.9 4.0 collective-permute-start.14
  84.1 5.6 %collective-permute-done.20.refs_1_ = f32[128,512]{1,0:T(8,128)S(1)} collective-permute-done((f32[128,512]{1,0:T(8,128)S(1)}, f32[128,512]{1,0:T(8,128)S(1)}, u32[]{:S(2)}, u32[]{:S(2)}) %collective-permute-start.20) | collective-permute-done | bytes 262176 | tf_op jit(solution)/shard_map/ppermute | solution.py:451
  89.7 2.0 gate.7
  93.0 6.0 %part.7 = (f32[128,4096]{1,0:T(8,128)S(1)}, f32[32,4096]{1,0:T(8,128)S(1)}, f32[32,4096]{1,0:T(8,128)S(1)}, f32[32,4096]{1,0:T(8,128)S(1)}, f32[32,4096]{1,0:T(8,128)S(1)}, /*index=5*/f32[8,128]{1,0:T(8,128)S(1)}) custom-call(f32[256,512]{1,0:T(8,128)S(1)} %bitcast.66, bf16[12,2,1024,512]{3,2,1,0:T(8,128)(2,1)} %get-tuple-element.233.refs_1_.refs_8_.refs_3_, ...), custom_call_target="tpu_custom_call" | custom-call | tf_op jit(solution)/shard_map/part/pallas_call | solution.py:89
  99.1 2.6 collective-permute-start.25
  102.3 11.6 %collective-permute-done.25.refs_2_ = f32[128,512]{1,0:T(8,128)S(1)} collective-permute-done((f32[128,512]{1,0:T(8,128)S(1)}, f32[128,512]{1,0:T(8,128)S(1)}, u32[]{:S(2)}, u32[]{:S(2)}) %collective-permute-start.25) | collective-permute-done | bytes 262176 | tf_op jit(solution)/shard_map/ppermute | solution.py:471
  113.9 8.2 %recon.7 = (f32[128,512]{1,0:T(8,128)S(1)}, f32[128,512]{1,0:T(8,128)S(1)}, bf16[2,1024,4096]{2,1,0:T(8,128)(2,1)}, f32[8,128]{1,0:T(8,128)S(1)}) custom-call(f32[16,4096]{1,0:T(8,128)S(1)} %get-tuple-element.272.refs_0_, f32[16,4096]{1,0:T(8,128)S(1)} %get-tuple-element.273.refs_1_, ...), custom_call_target="tpu_custom_call", output_to_operand_aliasing={{2}: (9, {})} | custom-call | tf_op jit(solution)/shard_map/recon/pallas_call | solution.py:89
  122.2 4.4 collective-permute-start.31
  129.0 3.8 collective-permute-done.31.refs_3_
  133.4 4.1 collective-permute-done.33.refs_2_
  137.5 11.4 %back.6 = (f32[64,4096]{1,0:T(8,128)S(1)}, f32[16,4096]{1,0:T(8,128)S(1)}, f32[16,4096]{1,0:T(8,128)S(1)}, f32[16,4096]{1,0:T(8,128)S(1)}, f32[16,4096]{1,0:T(8,...) custom-call(s32[2]{0:T(128)S(1)} %pad_add_fusion.refs_0_, f32[128,512]{1,0:T(8,128)S(1)} %get-tuple-element.285.refs_1_, ...), custom_call_target="tpu_custom_call" | custom-call | tf_op jit(solution)/shard_map/back/pallas_call | solution.py:89
  150.7 7.1 %collective-permute-done.32.refs_1_ = f32[128,512]{1,0:T(8,128)S(1)} collective-permute-done((f32[128,512]{1,0:T(8,128)S(1)}, f32[128,512]{1,0:T(8,128)S(1)}, u32[]{:S(2)}, u32[]{:S(2)}) %collective-permute-start.32) | collective-permute-done | bytes 262176 | tf_op jit(solution)/shard_map/ppermute | solution.py:451
  162.8 4.9 %part.8 = (f32[64,4096]{1,0:T(8,128)S(1)}, f32[16,4096]{1,0:T(8,128)S(1)}, f32[16,4096]{1,0:T(8,128)S(1)}, f32[16,4096]{1,0:T(8,128)S(1)}, f32[16,4096]{1,0:T(8,128)S(1)}, /*index=5*/f32[8,128]{1,0:T(8,128)S(1)}) custom-call(f32[128,512]{1,0:T(8,128)S(1)} %bitcast.69, bf16[12,2,1024,512]{3,2,1,0:T(8,128)(2,1)} %get-tuple-element.233.refs_1_.refs_8_.refs_3_, ...), custom_call_target="tpu_custom_call" | custom-call | tf_op jit(solution)/shard_map/part/pallas_call | solution.py:89
  167.7 2.4 collective-permute-start.34
  170.1 11.1 %recon.8 = (f32[256,512]{1,0:T(8,128)S(1)}, f32[256,512]{1,0:T(8,128)S(1)}, bf16[2,1024,4096]{2,1,0:T(8,128)(2,1)}, f32[8,128]{1,0:T(8,128)S(1)}) custom-call(f32[32,4096]{1,0:T(8,128)S(1)} %get-tuple-element.297.refs_0_, f32[32,4096]{1,0:T(8,128)S(1)} %get-tuple-element.298.refs_1_, ...), custom_call_target="tpu_custom_call", output_to_operand_aliasing={{2}: (9, {})} | custom-call | tf_op jit(solution)/shard_map/recon/pallas_call | solution.py:89
  185.2 9.4 %collective-permute-done.45.refs_3_ = f32[256,512]{1,0:T(8,128)S(1)} collective-permute-done((f32[256,512]{1,0:T(8,128)S(1)}, f32[256,512]{1,0:T(8,128)S(1)}, u32[]{:S(2)}, u32[]{:S(2)}) %collective-permute-start.45) | collective-permute-done | bytes 524320 | tf_op jit(solution)/shard_map/ppermute | solution.py:433
  198.7 8.3 %collective-permute-done.44.refs_2_ = f32[128,512]{1,0:T(8,128)S(1)} collective-permute-done((f32[128,512]{1,0:T(8,128)S(1)}, f32[128,512]{1,0:T(8,128)S(1)}, u32[]{:S(2)}, u32[]{:S(2)}) %collective-permute-start.44) | collective-permute-done | bytes 262176 | tf_op jit(solution)/shard_map/ppermute | solution.py:488
  207.0 11.4 %back.7 = (f32[64,4096]{1,0:T(8,128)S(1)}, f32[16,4096]{1,0:T(8,128)S(1)}, f32[16,4096]{1,0:T(8,128)S(1)}, f32[16,4096]{1,0:T(8,128)S(1)}, f32[16,4096]{1,0:T(8,...) custom-call(s32[2]{0:T(128)S(1)} %pad_add_fusion.refs_0_, ...), custom_call_target="tpu_custom_call", output_to_operand_aliasing={{5}: (4, {})} | custom-call | tf_op jit(solution)/shard_map/back/pallas_call | solution.py:89
  221.8 2.5 gate.9
  225.6 4.9 %part.9 = (f32[64,4096]{1,0:T(8,128)S(1)}, f32[16,4096]{1,0:T(8,128)S(1)}, f32[16,4096]{1,0:T(8,128)S(1)}, f32[16,4096]{1,0:T(8,128)S(1)}, f32[16,4096]{1,0:T(8,128)S(1)}, /*index=5*/f32[8,128]{1,0:T(8,128)S(1)}) custom-call(f32[128,512]{1,0:T(8,128)S(1)} %bitcast.70, bf16[12,2,1024,512]{3,2,1,0:T(8,128)(2,1)} %get-tuple-element.233.refs_1_.refs_8_.refs_3_, ...), custom_call_target="tpu_custom_call" | custom-call | tf_op jit(solution)/shard_map/part/pallas_call | solution.py:89
  230.6 11.0 %recon.9 = (f32[256,512]{1,0:T(8,128)S(1)}, f32[256,512]{1,0:T(8,128)S(1)}, bf16[2,1024,4096]{2,1,0:T(8,128)(2,1)}, f32[8,128]{1,0:T(8,128)S(1)}) custom-call(f32[32,4096]{1,0:T(8,128)S(1)} %get-tuple-element.333.refs_0_, f32[32,4096]{1,0:T(8,128)S(1)} %get-tuple-element.334.refs_1_, ...), custom_call_target="tpu_custom_call", output_to_operand_aliasing={{2}: (9, {})} | custom-call | tf_op jit(solution)/shard_map/recon/pallas_call | solution.py:89
  241.6 1.9 collective-permute-start.65
  244.2 7.1 %collective-permute-done.59.refs_2_ = f32[256,512]{1,0:T(8,128)S(1)} collective-permute-done((f32[256,512]{1,0:T(8,128)S(1)}, f32[256,512]{1,0:T(8,128)S(1)}, u32[]{:S(2)}, u32[]{:S(2)}) %collective-permute-start.59) | collective-permute-done | bytes 524320 | tf_op jit(solution)/shard_map/ppermute | solution.py:471
  257.3 10.8 %collective-permute-done.67.refs_2_ = f32[256,512]{1,0:T(8,128)S(1)} collective-permute-done((f32[256,512]{1,0:T(8,128)S(1)}, f32[256,512]{1,0:T(8,128)S(1)}, u32[]{:S(2)}, u32[]{:S(2)}) %collective-permute-start.67) | collective-permute-done | bytes 524320 | tf_op jit(solution)/shard_map/ppermute | solution.py:488
  268.1 10.9 %back.8 = (f32[128,4096]{1,0:T(8,128)S(1)}, f32[32,4096]{1,0:T(8,128)S(1)}, f32[32,4096]{1,0:T(8,128)S(1)}, f32[32,4096]{1,0:T(8,128)S(1)}, f32[32,4096]{1,0:T(8...) custom-call(s32[2]{0:T(128)S(1)} %pad_add_fusion.refs_0_, ...), custom_call_target="tpu_custom_call", output_to_operand_aliasing={{5}: (4, {})} | custom-call | tf_op jit(solution)/shard_map/back/pallas_call | solution.py:89
  287.8 8.2 %recon.10 = (f32[128,512]{1,0:T(8,128)S(1)}, f32[128,512]{1,0:T(8,128)S(1)}, bf16[2,1024,4096]{2,1,0:T(8,128)(2,1)}, f32[8,128]{1,0:T(8,128)S(1)}) custom-call(f32[16,4096]{1,0:T(8,128)S(1)} %get-tuple-element.359.refs_0_, f32[16,4096]{1,0:T(8,128)S(1)} %get-tuple-element.360.refs_1_, ...), custom_call_target="tpu_custom_call", output_to_operand_aliasing={{2}: (9, {})} | custom-call | tf_op jit(solution)/shard_map/recon/pallas_call | solution.py:89
  296.1 9.0 %collective-permute-done.68.refs_2_ = f32[256,512]{1,0:T(8,128)S(1)} collective-permute-done((f32[256,512]{1,0:T(8,128)S(1)}, f32[256,512]{1,0:T(8,128)S(1)}, u32[]{:S(2)}, u32[]{:S(2)}) %collective-permute-start.68) | collective-permute-done | bytes 524320 | tf_op jit(solution)/shard_map/ppermute | solution.py:471
  307.0 4.8 %collective-permute-start.79 = (f32[128,512]{1,0:T(8,128)S(1)}, f32[128,512]{1,0:T(8,128)S(1)}, u32[]{:S(2)}, u32[]{:S(2)}) collective-permute-start(f32[128,512]{1,0:T(8,128)S(1)} %get-tuple-element.369.refs_2_), channel_id=1, source_target_pairs={{0,16},{1,17},{2,18},{3,19},{4,20},{5,21},{6,22},{7,23},{8,24},{9,... | collective-permute-start | bytes 786440 | tf_op jit(solution)/shard_map/ppermute | solution.py:433
  313.3 3.8 collective-permute-done.79.refs_3_
  317.8 3.7 collective-permute-done.78.refs_2_
  321.5 10.9 %back.9 = (f32[128,4096]{1,0:T(8,128)S(1)}, f32[32,4096]{1,0:T(8,128)S(1)}, f32[32,4096]{1,0:T(8,128)S(1)}, f32[32,4096]{1,0:T(8,128)S(1)}, f32[32,4096]{1,0:T(8...) custom-call(s32[2]{0:T(128)S(1)} %pad_add_fusion.refs_0_, ...), custom_call_target="tpu_custom_call", output_to_operand_aliasing={{5}: (4, {})} | custom-call | tf_op jit(solution)/shard_map/back/pallas_call | solution.py:89
  342.3 8.3 %recon.11 = (f32[128,512]{1,0:T(8,128)S(1)}, f32[128,512]{1,0:T(8,128)S(1)}, bf16[2,1024,4096]{2,1,0:T(8,128)(2,1)}, f32[8,128]{1,0:T(8,128)S(1)}) custom-call(f32[16,4096]{1,0:T(8,128)S(1)} %get-tuple-element.381.refs_0_, f32[16,4096]{1,0:T(8,128)S(1)} %get-tuple-element.382.refs_1_, ...), custom_call_target="tpu_custom_call", output_to_operand_aliasing={{2}: (9, {})} | custom-call | tf_op jit(solution)/shard_map/recon/pallas_call | solution.py:89
  350.6 2.0 collective-permute-start.89
  352.6 2.5 collective-permute-done.91.refs_2_
  360.9 5.0 %collective-permute-done.93.refs_2_ = f32[128,512]{1,0:T(8,128)S(1)} collective-permute-done((f32[128,512]{1,0:T(8,128)S(1)}, f32[128,512]{1,0:T(8,128)S(1)}, u32[]{:S(2)}, u32[]{:S(2)}) %collective-permute-start.93) | collective-permute-done | bytes 262176 | tf_op jit(solution)/shard_map/ppermute | solution.py:488
  365.9 11.4 %back.10 = (f32[64,4096]{1,0:T(8,128)S(1)}, f32[16,4096]{1,0:T(8,128)S(1)}, f32[16,4096]{1,0:T(8,128)S(1)}, f32[16,4096]{1,0:T(8,128)S(1)}, f32[16,4096]{1,0:T(8...) custom-call(s32[2]{0:T(128)S(1)} %pad_add_fusion.refs_0_, ...), custom_call_target="tpu_custom_call", output_to_operand_aliasing={{5}: (4, {})} | custom-call | tf_op jit(solution)/shard_map/back/pallas_call | solution.py:89
  381.7 11.3 %collective-permute-done.94.refs_2_ = f32[128,512]{1,0:T(8,128)S(1)} collective-permute-done((f32[128,512]{1,0:T(8,128)S(1)}, f32[128,512]{1,0:T(8,128)S(1)}, u32[]{:S(2)}, u32[]{:S(2)}) %collective-permute-start.94) | collective-permute-done | bytes 262176 | tf_op jit(solution)/shard_map/ppermute | solution.py:471
  396.9 6.7 %collective-permute-done.100.refs_2_ = f32[128,512]{1,0:T(8,128)S(1)} collective-permute-done((f32[128,512]{1,0:T(8,128)S(1)}, f32[128,512]{1,0:T(8,128)S(1)}, u32[]{:S(2)}, u32[]{:S(2)}) %collective-permute-start.100) | collective-permute-done | bytes 262176 | tf_op jit(solution)/shard_map/ppermute | solution.py:488
  403.7 11.4 %back.11 = (f32[64,4096]{1,0:T(8,128)S(1)}, f32[16,4096]{1,0:T(8,128)S(1)}, f32[16,4096]{1,0:T(8,128)S(1)}, f32[16,4096]{1,0:T(8,128)S(1)}, f32[16,4096]{1,0:T(8...) custom-call(s32[2]{0:T(128)S(1)} %pad_add_fusion.refs_0_, ...), custom_call_target="tpu_custom_call", output_to_operand_aliasing={{5}: (4, {})} | custom-call | tf_op jit(solution)/shard_map/back/pallas_call | solution.py:89
  419.9 30.6 %decoder_grad.1 = (f32[1,2,4096,512]{3,2,1,0:T(8,128)}, f32[8,128]{1,0:T(8,128)S(1)}) custom-call(bf16[2,1024,4096]{2,1,0:T(8,128)(2,1)} %get-tuple-element.387.refs_0_, bf16[2,1024,1024]{2,1,0:T(8,128)(2,1)S(1)} %get-tuple-element.418.refs_1_, f32[8,128]{1,0:T(8,128)S(1)} %get-tuple-element.425.refs_2_), custom_call_target="tpu_custom_call" | custom-call | tf_op jit(solution)/shard_map/decoder_grad/pallas_call | solution.py:89
  452.8 1.8 collective-permute-done.106.refs_1_
  455.5 9.4 %collective-permute-done.105.refs_1_ = f32[32,4096]{1,0:T(8,128)S(1)} collective-permute-done((f32[32,4096]{1,0:T(8,128)S(1)}, f32[32,4096]{1,0:T(8,128)S(1)}, u32[]{:S(2)}, u32[]{:S(2)}) %collective-permute-start.105) | collective-permute-done | bytes 524320 | tf_op jit(solution)/shard_map/ppermute | solution.py:144
  (340 shorter events, 111.6 us)
Async XLA Ops:
  14.7 26.4 %collective-permute-start.9 = (f32[64,4096]{1,0:T(8,128)S(1)}, f32[64,4096]{1,0:T(8,128)S(1)}, u32[]{:S(2)}, u32[]{:S(2)}) collective-permute-start(f32[64,4096]{1,0:T(8,128)S(1)} %get-tuple-element.243.refs_1_), channel_id=1, source_target_pairs={{0,2},{1,3},{2,0},{3,1},{4,6},{5,7},{6,4},{7,5},{8,10},{9,11},{10,... | collective-permute-start | bytes 3145736 | tf_op jit(solution)/shard_map/ppermute | solution.py:144
  38.0 13.6 %collective-permute-start.15 = (f32[128,512]{1,0:T(8,128)S(1)}, f32[128,512]{1,0:T(8,128)S(1)}, u32[]{:S(2)}, u32[]{:S(2)}) collective-permute-start(f32[128,512]{1,0:T(8,128)S(1)} %get-tuple-element.254), channel_id=1, source_target_pairs={{0,16},{16,0},{1,17},{17,1},{2,18},{18,2},{3,19},{19,3},{4,20},{20... | collective-permute-start | bytes 786440 | tf_op jit(solution)/shard_map/ppermute | solution.py:336
  42.2 10.0 %collective-permute-start.11 = (f32[16,4096]{1,0:T(8,128)S(1)}, f32[16,4096]{1,0:T(8,128)S(1)}, u32[]{:S(2)}, u32[]{:S(2)}) collective-permute-start(f32[16,4096]{1,0:T(8,128)S(1)} %get-tuple-element.246.refs_1_), channel_id=1, source_target_pairs={{0,1},{1,0},{2,3},{3,2},{4,5},{5,4},{6,7},{7,6},{8,9},{9,8},{10,11... | collective-permute-start | bytes 786440 | tf_op jit(solution)/shard_map/ppermute | solution.py:141
  42.7 10.3 %collective-permute-start.12 = (f32[16,4096]{1,0:T(8,128)S(1)}, f32[16,4096]{1,0:T(8,128)S(1)}, u32[]{:S(2)}, u32[]{:S(2)}) collective-permute-start(f32[16,4096]{1,0:T(8,128)S(1)} %get-tuple-element.247.refs_2_), channel_id=1, source_target_pairs={{0,1},{1,0},{2,3},{3,2},{4,5},{5,4},{6,7},{7,6},{8,9},{9,8},{10,11... | collective-permute-start | bytes 786440 | tf_op jit(solution)/shard_map/ppermute | solution.py:141
  43.7 10.5 %collective-permute-start.13 = (f32[16,4096]{1,0:T(8,128)S(1)}, f32[16,4096]{1,0:T(8,128)S(1)}, u32[]{:S(2)}, u32[]{:S(2)}) collective-permute-start(f32[16,4096]{1,0:T(8,128)S(1)} %get-tuple-element.248.refs_3_), channel_id=1, source_target_pairs={{0,1},{1,0},{2,3},{3,2},{4,5},{5,4},{6,7},{7,6},{8,9},{9,8},{10,11... | collective-permute-start | bytes 786440 | tf_op jit(solution)/shard_map/ppermute | solution.py:141
  51.6 21.3 %collective-permute-start.16 = (f32[32,4096]{1,0:T(8,128)}, f32[32,4096]{1,0:T(8,128)S(1)}, u32[]{:S(2)}, u32[]{:S(2)}) collective-permute-start(f32[32,4096]{1,0:T(8,128)} %get-tuple-element.256), channel_id=1, source_target_pairs={{0,1},{1,0},{2,3},{3,2},{4,5},{5,4},{6,7},{7,6},{8,9},{9,8},{10,11... | collective-permute-start | bytes 1572872 | tf_op jit(solution)/shard_map/ppermute | solution.py:141
  51.8 25.2 %collective-permute-start.17 = (f32[32,4096]{1,0:T(8,128)}, f32[32,4096]{1,0:T(8,128)}, u32[]{:S(2)}, u32[]{:S(2)}) collective-permute-start(f32[32,4096]{1,0:T(8,128)} %get-tuple-element.257), channel_id=1, source_target_pairs={{0,1},{1,0},{2,3},{3,2},{4,5},{5,4},{6,7},{7,6},{8,9},{9,8},{10,11... | collective-permute-start | bytes 1572872 | tf_op jit(solution)/shard_map/ppermute | solution.py:141
  52.9 24.0 %collective-permute-start.18 = (f32[32,4096]{1,0:T(8,128)}, f32[32,4096]{1,0:T(8,128)}, u32[]{:S(2)}, u32[]{:S(2)}) collective-permute-start(f32[32,4096]{1,0:T(8,128)} %get-tuple-element.258), channel_id=1, source_target_pairs={{0,1},{1,0},{2,3},{3,2},{4,5},{5,4},{6,7},{7,6},{8,9},{9,8},{10,11... | collective-permute-start | bytes 1572872 | tf_op jit(solution)/shard_map/ppermute | solution.py:141
  53.7 23.2 %collective-permute-start.19 = (f32[32,4096]{1,0:T(8,128)}, f32[32,4096]{1,0:T(8,128)}, u32[]{:S(2)}, u32[]{:S(2)}) collective-permute-start(f32[32,4096]{1,0:T(8,128)} %get-tuple-element.259), channel_id=1, source_target_pairs={{0,1},{1,0},{2,3},{3,2},{4,5},{5,4},{6,7},{7,6},{8,9},{9,8},{10,11... | collective-permute-start | bytes 1572872 | tf_op jit(solution)/shard_map/ppermute | solution.py:141
  54.9 34.9 %collective-permute-start.8 = (f32[64,4096]{1,0:T(8,128)}, f32[64,4096]{1,0:T(8,128)}, u32[]{:S(2)}, u32[]{:S(2)}) collective-permute-start(f32[64,4096]{1,0:T(8,128)} %get-tuple-element.242.refs_1_), channel_id=1, source_target_pairs={{0,2},{1,3},{2,0},{3,1},{4,6},{5,7},{6,4},{7,5},{8,10},{9,11},{10,... | collective-permute-start | bytes 3145736 | tf_op jit(solution)/shard_map/ppermute | solution.py:144
  78.6 81.6 %collective-permute-start.35 = (f32[128,4096]{1,0:T(8,128)S(1)}, f32[128,4096]{1,0:T(8,128)S(1)}, u32[]{:S(2)}, u32[]{:S(2)}) collective-permute-start(f32[128,4096]{1,0:T(8,128)S(1)} %get-tuple-element.289.refs_1_), channel_id=1, source_target_pairs={{0,2},{1,3},{2,0},{3,1},{4,6},{5,7},{6,4},{7,5},{8,10},{9,11},{10,... | collective-permute-start | bytes 6291464 | tf_op jit(solution)/shard_map/ppermute | solution.py:144
  91.9 9.8 %collective-permute-start.27 = (f32[16,4096]{1,0:T(8,128)S(1)}, f32[16,4096]{1,0:T(8,128)S(1)}, u32[]{:S(2)}, u32[]{:S(2)}) collective-permute-start(f32[16,4096]{1,0:T(8,128)S(1)} %get-tuple-element.273.refs_1_), channel_id=1, source_target_pairs={{0,1},{1,0},{2,3},{3,2},{4,5},{5,4},{6,7},{7,6},{8,9},{9,8},{10,11... | collective-permute-start | bytes 786440 | tf_op jit(solution)/shard_map/ppermute | solution.py:141
  92.5 9.7 %collective-permute-start.29 = (f32[16,4096]{1,0:T(8,128)S(1)}, f32[16,4096]{1,0:T(8,128)S(1)}, u32[]{:S(2)}, u32[]{:S(2)}) collective-permute-start(f32[16,4096]{1,0:T(8,128)S(1)} %get-tuple-element.275.refs_3_), channel_id=1, source_target_pairs={{0,1},{1,0},{2,3},{3,2},{4,5},{5,4},{6,7},{7,6},{8,9},{9,8},{10,11... | collective-permute-start | bytes 786440 | tf_op jit(solution)/shard_map/ppermute | solution.py:141
  99.1 14.9 %collective-permute-start.25 = (f32[128,512]{1,0:T(8,128)S(1)}, f32[128,512]{1,0:T(8,128)S(1)}, u32[]{:S(2)}, u32[]{:S(2)}) collective-permute-start(f32[128,512]{1,0:T(8,128)S(1)} %get-tuple-element.271.refs_1_), channel_id=1, source_target_pairs={{0,8},{4,12},{8,0},{12,4},{1,9},{5,13},{9,1},{13,5},{2,10},{6,14},... | collective-permute-start | bytes 786440 | tf_op jit(solution)/shard_map/ppermute | solution.py:471
  101.7 20.4 %collective-permute-start.21 = (f32[32,4096]{1,0:T(8,128)S(1)}, f32[32,4096]{1,0:T(8,128)S(1)}, u32[]{:S(2)}, u32[]{:S(2)}) collective-permute-start(f32[32,4096]{1,0:T(8,128)S(1)} %get-tuple-element.267), channel_id=1, source_target_pairs={{0,1},{1,0},{2,3},{3,2},{4,5},{5,4},{6,7},{7,6},{8,9},{9,8},{10,11... | collective-permute-start | bytes 1572872 | tf_op jit(solution)/shard_map/ppermute | solution.py:141
  101.7 25.4 %collective-permute-start.22 = (f32[32,4096]{1,0:T(8,128)S(1)}, f32[32,4096]{1,0:T(8,128)S(1)}, u32[]{:S(2)}, u32[]{:S(2)}) collective-permute-start(f32[32,4096]{1,0:T(8,128)S(1)} %get-tuple-element.268), channel_id=1, source_target_pairs={{0,1},{1,0},{2,3},{3,2},{4,5},{5,4},{6,7},{7,6},{8,9},{9,8},{10,11... | collective-permute-start | bytes 1572872 | tf_op jit(solution)/shard_map/ppermute | solution.py:141
  102.2 26.5 %collective-permute-start.23 = (f32[32,4096]{1,0:T(8,128)S(1)}, f32[32,4096]{1,0:T(8,128)S(1)}, u32[]{:S(2)}, u32[]{:S(2)}) collective-permute-start(f32[32,4096]{1,0:T(8,128)S(1)} %get-tuple-element.269), channel_id=1, source_target_pairs={{0,1},{1,0},{2,3},{3,2},{4,5},{5,4},{6,7},{7,6},{8,9},{9,8},{10,11... | collective-permute-start | bytes 1572872 | tf_op jit(solution)/shard_map/ppermute | solution.py:141
  113.9 14.8 %collective-permute-start.24 = (f32[32,4096]{1,0:T(8,128)S(1)}, f32[32,4096]{1,0:T(8,128)S(1)}, u32[]{:S(2)}, u32[]{:S(2)}) collective-permute-start(f32[32,4096]{1,0:T(8,128)S(1)} %get-tuple-element.270), channel_id=1, source_target_pairs={{0,1},{1,0},{2,3},{3,2},{4,5},{5,4},{6,7},{7,6},{8,9},{9,8},{10,11... | collective-permute-start | bytes 1572872 | tf_op jit(solution)/shard_map/ppermute | solution.py:141
  122.2 10.6 %collective-permute-start.31 = (f32[128,512]{1,0:T(8,128)S(1)}, f32[128,512]{1,0:T(8,128)S(1)}, u32[]{:S(2)}, u32[]{:S(2)}) collective-permute-start(f32[128,512]{1,0:T(8,128)S(1)} %get-tuple-element.282.refs_2_), channel_id=1, source_target_pairs={{0,16},{1,17},{2,18},{3,19},{4,20},{5,21},{6,22},{7,23},{8,24},{9,... | collective-permute-start | bytes 786440 | tf_op jit(solution)/shard_map/ppermute | solution.py:433
  127.2 10.3 %collective-permute-start.33 = (f32[128,512]{1,0:T(8,128)S(1)}, f32[128,512]{1,0:T(8,128)S(1)}, u32[]{:S(2)}, u32[]{:S(2)}) collective-permute-start(f32[128,512]{1,0:T(8,128)S(1)} %get-tuple-element.285.refs_1_), channel_id=1, source_target_pairs={{16,0},{17,1},{18,2},{19,3},{20,4},{21,5},{22,6},{23,7},{24,8},{25... | collective-permute-start | bytes 786440 | tf_op jit(solution)/shard_map/ppermute | solution.py:488
  157.7 64.1 %collective-permute-start.30 = (f32[128,4096]{1,0:T(8,128)S(1)}, f32[128,4096]{1,0:T(8,128)}, u32[]{:S(2)}, u32[]{:S(2)}) collective-permute-start(f32[128,4096]{1,0:T(8,128)S(1)} %get-tuple-element.280.refs_1_), channel_id=1, source_target_pairs={{0,2},{1,3},{2,0},{3,1},{4,6},{5,7},{6,4},{7,5},{8,10},{9,11},{10,... | collective-permute-start | bytes 6291464 | tf_op jit(solution)/shard_map/ppermute | solution.py:144
  167.7 15.4 %collective-permute-start.34 = (f32[128,512]{1,0:T(8,128)S(1)}, f32[128,512]{1,0:T(8,128)S(1)}, u32[]{:S(2)}, u32[]{:S(2)}) collective-permute-start(f32[128,512]{1,0:T(8,128)S(1)} %get-tuple-element.288.refs_1_), channel_id=1, source_target_pairs={{0,8},{4,12},{8,0},{12,4},{1,9},{5,13},{9,1},{13,5},{2,10},{6,14},... | collective-permute-start | bytes 786440 | tf_op jit(solution)/shard_map/ppermute | solution.py:471
  170.1 13.2 %collective-permute-start.46 = (f32[16,4096]{1,0:T(8,128)S(1)}, f32[16,4096]{1,0:T(8,128)S(1)}, u32[]{:S(2)}, u32[]{:S(2)}) collective-permute-start(f32[16,4096]{1,0:T(8,128)S(1)} %get-tuple-element.310), channel_id=1, source_target_pairs={{0,1},{1,0},{2,3},{3,2},{4,5},{5,4},{6,7},{7,6},{8,9},{9,8},{10,11... | collective-permute-start | bytes 786440 | tf_op jit(solution)/shard_map/ppermute | solution.py:141
  181.2 13.4 %collective-permute-start.45 = (f32[256,512]{1,0:T(8,128)S(1)}, f32[256,512]{1,0:T(8,128)S(1)}, u32[]{:S(2)}, u32[]{:S(2)}) collective-permute-start(f32[256,512]{1,0:T(8,128)S(1)} %get-tuple-element.308.refs_2_), channel_id=1, source_target_pairs={{0,16},{1,17},{2,18},{3,19},{4,20},{5,21},{6,22},{7,23},{8,24},{9,... | collective-permute-start | bytes 1572872 | tf_op jit(solution)/shard_map/ppermute | solution.py:433
  195.3 23.7 %collective-permute-start.54 = (f32[256,512]{1,0:T(8,128)S(1)}, f32[256,512]{1,0:T(8,128)S(1)}, u32[]{:S(2)}, u32[]{:S(2)}) collective-permute-start(f32[256,512]{1,0:T(8,128)S(1)} %get-tuple-element.322.refs_0_), channel_id=1, source_target_pairs={{0,4},{4,0},{8,12},{12,8},{1,5},{5,1},{9,13},{13,9},{2,6},{6,2},{1... | collective-permute-start | bytes 1572872 | tf_op jit(solution)/shard_map/ppermute | solution.py:451
  197.2 9.8 %collective-permute-start.44 = (f32[128,512]{1,0:T(8,128)S(1)}, f32[128,512]{1,0:T(8,128)S(1)}, u32[]{:S(2)}, u32[]{:S(2)}) collective-permute-start(f32[128,512]{1,0:T(8,128)S(1)} %get-tuple-element.305.refs_1_), channel_id=1, source_target_pairs={{16,0},{17,1},{18,2},{19,3},{20,4},{21,5},{22,6},{23,7},{24,8},{25... | collective-permute-start | bytes 786440 | tf_op jit(solution)/shard_map/ppermute | solution.py:488
  225.4 25.8 %collective-permute-start.59 = (f32[256,512]{1,0:T(8,128)S(1)}, f32[256,512]{1,0:T(8,128)S(1)}, u32[]{:S(2)}, u32[]{:S(2)}) collective-permute-start(f32[256,512]{1,0:T(8,128)S(1)} %get-tuple-element.332.refs_1_), channel_id=1, source_target_pairs={{0,8},{4,12},{8,0},{12,4},{1,9},{5,13},{9,1},{13,5},{2,10},{6,14},... | collective-permute-start | bytes 1572872 | tf_op jit(solution)/shard_map/ppermute | solution.py:471
  241.6 12.9 %collective-permute-start.65 = (f32[256,512]{1,0:T(8,128)S(1)}, f32[256,512]{1,0:T(8,128)S(1)}, u32[]{:S(2)}, u32[]{:S(2)}) collective-permute-start(f32[256,512]{1,0:T(8,128)S(1)} %get-tuple-element.343.refs_2_), channel_id=1, source_target_pairs={{0,16},{1,17},{2,18},{3,19},{4,20},{5,21},{6,22},{7,23},{8,24},{9,... | collective-permute-start | bytes 1572872 | tf_op jit(solution)/shard_map/ppermute | solution.py:433
  243.6 9.7 %collective-permute-start.56 = (f32[16,4096]{1,0:T(8,128)S(1)}, f32[16,4096]{1,0:T(8,128)S(1)}, u32[]{:S(2)}, u32[]{:S(2)}) collective-permute-start(f32[16,4096]{1,0:T(8,128)S(1)} %get-tuple-element.329), channel_id=1, source_target_pairs={{0,1},{1,0},{2,3},{3,2},{4,5},{5,4},{6,7},{7,6},{8,9},{9,8},{10,11... | collective-permute-start | bytes 786440 | tf_op jit(solution)/shard_map/ppermute | solution.py:141
  251.9 16.2 %collective-permute-start.67 = (f32[256,512]{1,0:T(8,128)S(1)}, f32[256,512]{1,0:T(8,128)S(1)}, u32[]{:S(2)}, u32[]{:S(2)}) collective-permute-start(f32[256,512]{1,0:T(8,128)S(1)} %get-tuple-element.346.refs_1_), channel_id=1, source_target_pairs={{16,0},{17,1},{18,2},{19,3},{20,4},{21,5},{22,6},{23,7},{24,8},{25... | collective-permute-start | bytes 1572872 | tf_op jit(solution)/shard_map/ppermute | solution.py:488
  255.2 24.5 %collective-permute-start.66 = (f32[256,512]{1,0:T(8,128)S(1)}, f32[256,512]{1,0:T(8,128)S(1)}, u32[]{:S(2)}, u32[]{:S(2)}) collective-permute-start(f32[256,512]{1,0:T(8,128)S(1)} %get-tuple-element.345.refs_0_), channel_id=1, source_target_pairs={{0,4},{4,0},{8,12},{12,8},{1,5},{5,1},{9,13},{13,9},{2,6},{6,2},{1... | collective-permute-start | bytes 1572872 | tf_op jit(solution)/shard_map/ppermute | solution.py:451
  255.9 28.1 %collective-permute-start.69 = (f32[64,4096]{1,0:T(8,128)S(1)}, f32[64,4096]{1,0:T(8,128)S(1)}, u32[]{:S(2)}, u32[]{:S(2)}) collective-permute-start(f32[64,4096]{1,0:T(8,128)S(1)} %get-tuple-element.351.refs_1_), channel_id=1, source_target_pairs={{0,2},{1,3},{2,0},{3,1},{4,6},{5,7},{6,4},{7,5},{8,10},{9,11},{10,... | collective-permute-start | bytes 3145736 | tf_op jit(solution)/shard_map/ppermute | solution.py:144
  281.0 24.1 %collective-permute-start.68 = (f32[256,512]{1,0:T(8,128)S(1)}, f32[256,512]{1,0:T(8,128)S(1)}, u32[]{:S(2)}, u32[]{:S(2)}) collective-permute-start(f32[256,512]{1,0:T(8,128)S(1)} %get-tuple-element.350.refs_1_), channel_id=1, source_target_pairs={{0,8},{4,12},{8,0},{12,4},{1,9},{5,13},{9,1},{13,5},{2,10},{6,14},... | collective-permute-start | bytes 1572872 | tf_op jit(solution)/shard_map/ppermute | solution.py:471
  305.7 15.8 %collective-permute-start.78 = (f32[256,512]{1,0:T(8,128)S(1)}, f32[256,512]{1,0:T(8,128)S(1)}, u32[]{:S(2)}, u32[]{:S(2)}) collective-permute-start(f32[256,512]{1,0:T(8,128)S(1)} %get-tuple-element.366.refs_1_), channel_id=1, source_target_pairs={{16,0},{17,1},{18,2},{19,3},{20,4},{21,5},{22,6},{23,7},{24,8},{25... | collective-permute-start | bytes 1572872 | tf_op jit(solution)/shard_map/ppermute | solution.py:488
  307.0 10.0 %collective-permute-start.79 = (f32[128,512]{1,0:T(8,128)S(1)}, f32[128,512]{1,0:T(8,128)S(1)}, u32[]{:S(2)}, u32[]{:S(2)}) collective-permute-start(f32[128,512]{1,0:T(8,128)S(1)} %get-tuple-element.369.refs_2_), channel_id=1, source_target_pairs={{0,16},{1,17},{2,18},{3,19},{4,20},{5,21},{6,22},{7,23},{8,24},{9,... | collective-permute-start | bytes 786440 | tf_op jit(solution)/shard_map/ppermute | solution.py:433
  311.8 25.6 %collective-permute-start.64 = (f32[64,4096]{1,0:T(8,128)S(1)}, f32[64,4096]{1,0:T(8,128)S(1)}, u32[]{:S(2)}, u32[]{:S(2)}) collective-permute-start(f32[64,4096]{1,0:T(8,128)S(1)} %get-tuple-element.341.refs_1_), channel_id=1, source_target_pairs={{0,2},{1,3},{2,0},{3,1},{4,6},{5,7},{6,4},{7,5},{8,10},{9,11},{10,... | collective-permute-start | bytes 3145736 | tf_op jit(solution)/shard_map/ppermute | solution.py:144
  317.7 15.3 %collective-permute-start.84 = (f32[128,512]{1,0:T(8,128)S(1)}, f32[128,512]{1,0:T(8,128)S(1)}, u32[]{:S(2)}, u32[]{:S(2)}) collective-permute-start(f32[128,512]{1,0:T(8,128)S(1)} %get-tuple-element.377.refs_0_), channel_id=1, source_target_pairs={{0,4},{4,0},{8,12},{12,8},{1,5},{5,1},{9,13},{13,9},{2,6},{6,2},{1... | collective-permute-start | bytes 786440 | tf_op jit(solution)/shard_map/ppermute | solution.py:451
  338.6 18.7 %collective-permute-start.90 = (f32[32,4096]{1,0:T(8,128)S(1)}, f32[32,4096]{1,0:T(8,128)S(1)}, u32[]{:S(2)}, u32[]{:S(2)}) collective-permute-start(f32[32,4096]{1,0:T(8,128)S(1)} %get-tuple-element.391), channel_id=1, source_target_pairs={{0,2},{1,3},{2,0},{3,1},{4,6},{5,7},{6,4},{7,5},{8,10},{9,11},{10,... | collective-permute-start | bytes 1572872 | tf_op jit(solution)/shard_map/ppermute | solution.py:144
  340.6 14.5 %collective-permute-start.91 = (f32[128,512]{1,0:T(8,128)S(1)}, f32[128,512]{1,0:T(8,128)S(1)}, u32[]{:S(2)}, u32[]{:S(2)}) collective-permute-start(f32[128,512]{1,0:T(8,128)S(1)} %get-tuple-element.393.refs_1_), channel_id=1, source_target_pairs={{0,8},{4,12},{8,0},{12,4},{1,9},{5,13},{9,1},{13,5},{2,10},{6,14},... | collective-permute-start | bytes 786440 | tf_op jit(solution)/shard_map/ppermute | solution.py:471
  355.7 10.2 %collective-permute-start.93 = (f32[128,512]{1,0:T(8,128)S(1)}, f32[128,512]{1,0:T(8,128)S(1)}, u32[]{:S(2)}, u32[]{:S(2)}) collective-permute-start(f32[128,512]{1,0:T(8,128)S(1)} %get-tuple-element.398.refs_1_), channel_id=1, source_target_pairs={{16,0},{17,1},{18,2},{19,3},{20,4},{21,5},{22,6},{23,7},{24,8},{25... | collective-permute-start | bytes 786440 | tf_op jit(solution)/shard_map/ppermute | solution.py:488
  359.1 18.9 %collective-permute-start.92 = (f32[128,512]{1,0:T(8,128)S(1)}, f32[128,512]{1,0:T(8,128)S(1)}, u32[]{:S(2)}, u32[]{:S(2)}) collective-permute-start(f32[128,512]{1,0:T(8,128)S(1)} %get-tuple-element.397.refs_0_), channel_id=1, source_target_pairs={{0,4},{4,0},{8,12},{12,8},{1,5},{5,1},{9,13},{13,9},{2,6},{6,2},{1... | collective-permute-start | bytes 786440 | tf_op jit(solution)/shard_map/ppermute | solution.py:451
  360.2 20.5 %collective-permute-start.95 = (f32[32,4096]{1,0:T(8,128)S(1)}, f32[32,4096]{1,0:T(8,128)S(1)}, u32[]{:S(2)}, u32[]{:S(2)}) collective-permute-start(f32[32,4096]{1,0:T(8,128)S(1)} %get-tuple-element.404), channel_id=1, source_target_pairs={{0,2},{1,3},{2,0},{3,1},{4,6},{5,7},{6,4},{7,5},{8,10},{9,11},{10,... | collective-permute-start | bytes 1572872 | tf_op jit(solution)/shard_map/ppermute | solution.py:144
  378.9 14.0 %collective-permute-start.94 = (f32[128,512]{1,0:T(8,128)S(1)}, f32[128,512]{1,0:T(8,128)S(1)}, u32[]{:S(2)}, u32[]{:S(2)}) collective-permute-start(f32[128,512]{1,0:T(8,128)S(1)} %get-tuple-element.402.refs_1_), channel_id=1, source_target_pairs={{0,8},{4,12},{8,0},{12,4},{1,9},{5,13},{9,1},{13,5},{2,10},{6,14},... | collective-permute-start | bytes 786440 | tf_op jit(solution)/shard_map/ppermute | solution.py:471
  393.5 10.1 %collective-permute-start.100 = (f32[128,512]{1,0:T(8,128)S(1)}, f32[128,512]{1,0:T(8,128)S(1)}, u32[]{:S(2)}, u32[]{:S(2)}) collective-permute-start(f32[128,512]{1,0:T(8,128)S(1)} %get-tuple-element.415.refs_1_), channel_id=1, source_target_pairs={{16,0},{17,1},{18,2},{19,3},{20,4},{21,5},{22,6},{23,7},{24,8},{25... | collective-permute-start | bytes 786440 | tf_op jit(solution)/shard_map/ppermute | solution.py:488
  394.8 55.7 %collective-permute-start.108 = (f32[64,4096]{1,0:T(8,128)S(1)}, f32[64,4096]{1,0:T(8,128)S(1)}, u32[]{:S(2)}, u32[]{:S(2)}) collective-permute-start(f32[64,4096]{1,0:T(8,128)S(1)} %get-tuple-element.437), channel_id=1, source_target_pairs={{0,2},{1,3},{2,0},{3,1},{4,6},{5,7},{6,4},{7,5},{8,10},{9,11},{10,... | collective-permute-start | bytes 3145736 | tf_op jit(solution)/shard_map/ppermute | solution.py:144
  395.5 56.1 %collective-permute-start.107 = (f32[64,4096]{1,0:T(8,128)S(1)}, f32[64,4096]{1,0:T(8,128)S(1)}, u32[]{:S(2)}, u32[]{:S(2)}) collective-permute-start(f32[64,4096]{1,0:T(8,128)S(1)} %get-tuple-element.434), channel_id=1, source_target_pairs={{0,2},{1,3},{2,0},{3,1},{4,6},{5,7},{6,4},{7,5},{8,10},{9,11},{10,... | collective-permute-start | bytes 3145736 | tf_op jit(solution)/shard_map/ppermute | solution.py:144
  417.1 37.6 %collective-permute-start.106 = (f32[32,4096]{1,0:T(8,128)S(1)}, f32[32,4096]{1,0:T(8,128)S(1)}, u32[]{:S(2)}, u32[]{:S(2)}) collective-permute-start(f32[32,4096]{1,0:T(8,128)S(1)} %get-tuple-element.431), channel_id=1, source_target_pairs={{0,2},{1,3},{2,0},{3,1},{4,6},{5,7},{6,4},{7,5},{8,10},{9,11},{10,... | collective-permute-start | bytes 1572872 | tf_op jit(solution)/shard_map/ppermute | solution.py:144
  418.9 46.0 %collective-permute-start.105 = (f32[32,4096]{1,0:T(8,128)S(1)}, f32[32,4096]{1,0:T(8,128)S(1)}, u32[]{:S(2)}, u32[]{:S(2)}) collective-permute-start(f32[32,4096]{1,0:T(8,128)S(1)} %get-tuple-element.428), channel_id=1, source_target_pairs={{0,2},{1,3},{2,0},{3,1},{4,6},{5,7},{6,4},{7,5},{8,10},{9,11},{10,... | collective-permute-start | bytes 1572872 | tf_op jit(solution)/shard_map/ppermute | solution.py:144
  (100 other events, 575.5 us)

commit v2 on v1

--- a/solution.py
+++ b/solution.py
@@ -8,7 +8,7 @@
 from jax.sharding import PartitionSpec as P
 
 softness = 0.5
-eighths = (1, 1, 2, 2, 1, 1)
+eighths = (1, 2, 2, 2, 1)
 cuts = 4
 f32 = jnp.float32
 bf16 = jnp.bfloat16
@@ -16,7 +16,7 @@
 scalars = pl.BlockSpec(memory_space=pltpu.SMEM)
 vector = pl.BlockSpec(memory_space=pltpu.VMEM)
 hbm = pl.BlockSpec(memory_space=pltpu.HBM)
-granted = 46 * 1024 * 1024
+mega = 1024 * 1024
 
 
 def pieces_of(rows):
@@ -66,7 +66,7 @@
         self.last = None
 
     def __call__(
-        self, name, body, inputs, outputs, scratch=(), aliases=None, grid=None
+        self, name, body, inputs, outputs, scratch=(), aliases=None, limit=16, grid=None
     ):
         arrays = [a for a, _ in inputs]
         in_specs = [s for _, s in inputs]
@@ -94,7 +94,7 @@
             out_shape=[o for o, _ in outputs] + [shape((8, 128))],
             scratch_shapes=list(scratch),
             input_output_aliases=aliases or {},
-            compiler_params=pltpu.CompilerParams(vmem_limit_bytes=granted),
+            compiler_params=pltpu.CompilerParams(vmem_limit_bytes=limit * mega),
             cost_estimate=pl.CostEstimate(flops=0, bytes_accessed=0, transcendentals=0),
             name=name,
         )(*arrays)
@@ -125,13 +125,8 @@
     feats = w_enc.shape[2]
     share = tokens // width
     tile = min(512, feats)
+    tiles = feats // tile
     wide = min(1024, feats)
-    wides = feats // wide
-    group = min(model, wide)
-    groups = wide // group
-    shared = (groups * model, group) == (wide, model)
-    blocks = 3 * wides if shared else wides
-    skipped = wides if shared else 0
     near_pairs = [(i, i ^ 1) for i in range(width)]
     far_pairs = [(i, i ^ 2) for i in range(width)]
     pieces = pieces_of(share)
@@ -175,86 +170,59 @@
             start = 2 * n + k * cut_rows(i)
             out[:, columns] = value[start : start + cut_rows(i)]
 
-    def fetch(source, buffers, sems):
-        return lambda k: pltpu.make_async_copy(source.at[k], buffers.at[k % 2], sems.at[k % 2])
-
-    def fetch_pairs(source, buffers, sems):
-        return lambda k: pltpu.make_async_copy(
-            source.at[pl.ds(skipped + 2 * k, 2)], buffers.at[k % 2], sems.at[k % 2]
-        )
-
     def enter(i):
         n = size(i)
 
-        def body(ins, outs, buffers, made, sems):
+        def body(ins, outs, buffers, sems):
             x, w = ins
-            own, *others, kept = outs
+            own, *others, high, low = outs
             x_high, x_low = halves(x[...])
 
             def read(k):
                 return pltpu.make_async_copy(
-                    w.at[0, :, pl.ds(k * wide, wide)], buffers.at[k % 2], sems.at[k % 2]
+                    w.at[0, :, pl.ds(k * tile, tile)], buffers.at[k % 2], sems.at[k % 2]
                 )
 
-            def write(k):
-                return pltpu.make_async_copy(made.at[k % 2], kept.at[k], sems.at[2 + k % 2])
-
             def step(k, slot):
+                columns = slice(k * tile, (k + 1) * tile)
                 w_high, w_low = halves(buffers[slot])
-                if k >= 2:
-                    write(k - 2).wait()
-                for g in range(groups):
-                    rows, cut = slice(g * model, (g + 1) * model), slice(g * group, (g + 1) * group)
-                    made[slot, 0, rows], made[slot, 1, rows] = w_high[:, cut], w_low[:, cut]
-                write(k).start()
-                columns = slice(k * wide, (k + 1) * wide)
+                high[:, columns], low[:, columns] = w_high, w_low
                 write_cuts(i, three(x_high, x_low, w_high, w_low, plain), own, others, columns)
 
-            stream(wides, read, step)
-            for k in range(max(wides - 2, 0), wides):
-                write(k).wait()
-
-        own, *others, weights["enc"] = chain(
+            stream(tiles, read, step)
+
+        own, *others, high, low = chain(
             "enter",
             body,
             [(x_rows[i], vector), (w_enc, hbm)],
             [(shape((2 * n, feats)), vector)]
             + cut_shapes(i)
-            + [(shape((blocks, 2, groups * model, group), bf16), hbm)],
-            scratch=[
-                pltpu.VMEM((2, model, wide), f32),
-                pltpu.VMEM((2, 2, groups * model, group), bf16),
-                pltpu.SemaphoreType.DMA((4,)),
-            ],
-        )
+            + [(shape((model, feats), bf16), vector)] * 2,
+            scratch=[pltpu.VMEM((2, model, tile), f32), pltpu.SemaphoreType.DMA((2,))],
+            limit=46,
+        )
+        weights["enc"] = [high, low]
         store[i]["own"], store[i]["in"] = own, swap_near(others)
 
     def part(i):
         n = size(i)
 
-        def body(ins, outs, buffers, sems):
-            x, w = ins
+        def body(ins, outs):
+            x, high, low = ins
             own, *others = outs
-
-            def step(k, slot):
-                x_high, x_low = halves(x[...])
-                for g in range(groups):
-                    rows = slice(g * model, (g + 1) * model)
-                    value = three(x_high, x_low, buffers[slot, 0, rows], buffers[slot, 1, rows], plain)
-                    start = k * wide + g * group
-                    write_cuts(i, value, own, others, slice(start, start + group))
-
-            stream(wides, fetch(w, buffers, sems), step)
+            x_high, x_low = halves(x[...])
+
+            def step(columns):
+                value = three(x_high, x_low, high[:, columns], low[:, columns], plain)
+                write_cuts(i, value, own, others, columns)
+
+            loop(feats, wide, step)
 
         own, *others = chain(
             "part",
             body,
-            [(x_rows[i], vector), (weights["enc"], hbm)],
+            [(x_rows[i], vector)] + [(w, vector) for w in weights["enc"]],
             [(shape((2 * n, feats)), vector)] + cut_shapes(i),
-            scratch=[
-                pltpu.VMEM((2, 2, groups * model, group), bf16),
-                pltpu.SemaphoreType.DMA((2,)),
-            ],
         )
         store[i]["own"], store[i]["in"] = own, swap_near(others)
 
@@ -278,44 +246,30 @@
         store[i]["sum"], store[i]["in"] = value, swap_far(value)
 
     def split_decoder():
-        def body(ins, outs, buffers, made, sems):
-            w, kept = ins[0], outs[0]
+        def body(ins, outs, buffers, sems):
+            w = ins[0]
+            high, low = outs
 
             def read(k):
                 return pltpu.make_async_copy(
-                    w.at[0, :, pl.ds(k * wide, wide)], buffers.at[k % 2], sems.at[k % 2]
+                    w.at[0, :, pl.ds(k * tile, tile)], buffers.at[k % 2], sems.at[k % 2]
                 )
 
-            def write(k):
-                return pltpu.make_async_copy(
-                    made.at[k % 2], kept.at[pl.ds(skipped + 2 * k, 2)], sems.at[2 + k % 2]
-                )
-
             def step(k, slot):
-                if k >= 2:
-                    write(k - 2).wait()
+                rows = slice(k * tile, (k + 1) * tile)
                 for t in range(2):
-                    made[slot, t, 0], made[slot, t, 1] = halves(buffers[slot, t])
-                write(k).start()
-
-            stream(wides, read, step)
-            for k in range(max(wides - 2, 0), wides):
-                write(k).wait()
-
-        (weights["dec"],) = chain(
+                    high[t, rows], low[t, rows] = halves(buffers[slot, t])
+
+            stream(tiles, read, step)
+
+        weights["dec"] = chain(
             "split_decoder",
             body,
-            [(w_dec, hbm)] + ([(weights["enc"], hbm)] if shared else []),
-            [(shape((skipped + 2 * wides, 2, wide, model), bf16), hbm)],
-            aliases={1: 0} if shared else {},
-            scratch=[
-                pltpu.VMEM((2, 2, wide, model), f32),
-                pltpu.VMEM((2, 2, 2, wide, model), bf16),
-                pltpu.SemaphoreType.DMA((4,)),
-            ],
-        )
-        if shared:
-            weights["enc"] = weights["dec"]
+            [(w_dec, hbm)],
+            [(shape((2, feats, model), bf16), vector)] * 2,
+            scratch=[pltpu.VMEM((2, 2, tile, model), f32), pltpu.SemaphoreType.DMA((2,))],
+            limit=28,
+        )
 
     def goals():
         share_rows = targets.shape[1]
@@ -379,54 +333,43 @@
         )
         store[i]["acts"], store[i]["slope"], store[i]["in"] = acts, slope, swap_near(acts)
 
-    def keep(name, ins, outs, columns):
+    def recon(i):
+        n = size(i)
+        lo = pieces[i][0]
+
+        def body(ins, outs, made, sem):
+            own, other = ins[:cuts], ins[cuts : 2 * cuts]
+            high, low = ins[2 * cuts : 2 * cuts + 2]
+            r0, r1, kept = outs
+            rows = pl.ds(4 * lo, 4 * n)
+            r0[...] = jnp.zeros_like(r0)
+            r1[...] = jnp.zeros_like(r1)
+
+            def step(columns):
+                a_high, a_low = halves(join(own + other, columns))
+                made[0, :, columns], made[1, :, columns] = a_high, a_low
+                pltpu.make_async_copy(
+                    made.at[:, :, columns], kept.at[pl.ds(0, 2), rows, columns], sem
+                ).start()
+                for t, out in enumerate((r0, r1)):
+                    out[...] += three(a_high, a_low, high[t, columns], low[t, columns], plain)
+
+            loop(feats, wide, step)
+            pltpu.make_async_copy(made, kept.at[pl.ds(0, 2), rows], sem).wait()
+
+        ins = [(a, vector) for a in [*store[i]["acts"], *store[i]["in"], *weights["dec"]]]
+        outs = [(shape((4 * n, model)), vector)] * 2
         aliases = {}
-        if name in saved:
+        if "acts" in saved:
             aliases = {len(ins): len(outs)}
-            ins.append((saved[name], hbm))
-        outs.append((shape((2, tokens, columns), bf16), hbm))
-        return aliases
-
-    def recon(i):
-        n = size(i)
-        lo = pieces[i][0]
-
-        def body(ins, outs, buffers, made, sems):
-            own, other, w = ins[:cuts], ins[cuts : 2 * cuts], ins[2 * cuts]
-            r0, r1, kept = outs
-
-            def save(k):
-                rows, columns = pl.ds(4 * lo, 4 * n), pl.ds(k * wide, wide)
-                return pltpu.make_async_copy(
-                    made.at[k % 2], kept.at[:, rows, columns], sems.at[2 + k % 2]
-                )
-
-            def step(k, slot):
-                columns = slice(k * wide, (k + 1) * wide)
-                a_high, a_low = halves(join(own + other, columns))
-                if k >= 2:
-                    save(k - 2).wait()
-                made[slot, 0], made[slot, 1] = a_high, a_low
-                save(k).start()
-                for t, out in enumerate((r0, r1)):
-                    value = three(a_high, a_low, buffers[slot, t, 0], buffers[slot, t, 1], plain)
-                    out[...] = out[...] + value if k else value
-
-            stream(wides, fetch_pairs(w, buffers, sems), step)
-            for k in range(max(wides - 2, 0), wides):
-                save(k).wait()
-
-        ins = [(a, vector) for a in [*store[i]["acts"], *store[i]["in"]]] + [(weights["dec"], hbm)]
-        outs = [(shape((4 * n, model)), vector)] * 2
-        aliases = keep("acts", ins, outs, feats)
+            ins.append((saved["acts"], hbm))
+        outs.append((shape((4, tokens, feats), bf16), hbm))
         r0, r1, saved["acts"] = chain(
             "recon",
             body,
             ins,
             outs,
-            scratch=[pltpu.VMEM((2, 2, 2, wide, model), bf16)]
-            + [pltpu.VMEM((2, 2, 4 * n, wide), bf16)]
-            + [pltpu.SemaphoreType.DMA((4,))],
+            scratch=[pltpu.VMEM((2, 4 * n, feats), bf16), pltpu.SemaphoreType.DMA],
             aliases=aliases,
         )
         store[i]["r"] = (r0, r1)
@@ -489,46 +432,33 @@
 
     def back(i):
         n = size(i)
-        lo = pieces[i][0]
-
-        def body(ins, outs, buffers, made, sems):
-            flag, value, above, w = ins[:4]
-            own, *others, kept = outs
-            e_high, e_low = made.at[0], made.at[1]
+
+        def body(ins, outs):
+            flag, value, above, high, low = ins
+            own, *others, e = outs
+            e_high, e_low = e.at[0], e.at[1]
             is_first = flag[0] == 1
             zero = jnp.where(is_first, value[...], 0.0)
             one = jnp.where(is_first, above[...], value[...])
             e_high[:, :model], e_low[:, :model] = halves(zero)
             e_high[:, model:], e_low[:, model:] = halves(one)
-            copy = pltpu.make_async_copy(made, kept.at[:, pl.ds(4 * lo, 4 * n)], sems.at[2])
-            copy.start()
-
-            def step(k, slot):
+            def step(columns):
                 total = None
                 for t in range(2):
                     cut = slice(t * model, (t + 1) * model)
-                    high, low = buffers[slot, t, 0], buffers[slot, t, 1]
-                    term = three(e_high[:, cut], e_low[:, cut], high, low, across_columns)
+                    term = three(
+                        e_high[:, cut], e_low[:, cut], high[t, columns], low[t, columns], across_columns
+                    )
                     total = term if total is None else total + term
-                write_cuts(i, total, own, others, slice(k * wide, (k + 1) * wide))
-
-            stream(wides, fetch_pairs(w, buffers, sems), step)
-            copy.wait()
-
-        arrays = [store[i]["held"], store[i]["in"]]
-        ins = [(flags, scalars)] + [(a, vector) for a in arrays] + [(weights["dec"], hbm)]
+                write_cuts(i, total, own, others, columns)
+
+            loop(feats, wide, step)
+
+        arrays = [store[i]["held"], store[i]["in"], *weights["dec"]]
+        ins = [(flags, scalars)] + [(a, vector) for a in arrays]
         outs = [(shape((2 * n, feats)), vector)] + cut_shapes(i)
-        aliases = keep("errors", ins, outs, 2 * model)
-        own, *others, saved["errors"] = chain(
-            "back",
-            body,
-            ins,
-            outs,
-            scratch=[pltpu.VMEM((2, 2, 2, wide, model), bf16)]
-            + [pltpu.VMEM((2, 4 * n, 2 * model), bf16)]
-            + [pltpu.SemaphoreType.DMA((3,))],
-            aliases=aliases,
-        )
+        outs.append((shape((2, 4 * n, 2 * model), bf16), vector))
+        own, *others, store[i]["errors"] = chain("back", body, ins, outs)
         store[i]["own"], store[i]["in"] = own, swap_near(others)
 
     def turn(i):
@@ -588,21 +518,28 @@
         )
 
     def decoder_grad():
-        def body(ins, outs):
-            a, e = ins
+        def body(ins, outs, e):
+            a, *errors = ins
+
+            @pl.when(pl.program_id(0) == 0)
+            def _():
+                for (lo, hi), piece in zip(pieces, errors):
+                    e[:, 4 * lo : 4 * hi] = piece[...]
+
             value = three(a[0], a[1], e[0], e[1], across_rows)
             outs[0][0, 0] = value[:, :model]
             outs[0][0, 1] = value[:, model:]
 
+        errors = [s["errors"] for s in store]
         (out,) = chain(
             "decoder_grad",
             body,
-            [
-                (saved["acts"], pl.BlockSpec((2, tokens, tile), lambda j: (0, 0, j))),
-                (saved["errors"], pl.BlockSpec((2, tokens, 2 * model), lambda j: (0, 0, 0))),
-            ],
+            [(saved["acts"], pl.BlockSpec((2, tokens, tile), lambda j: (0, 0, j)))]
+            + [(e, pl.BlockSpec(e.shape, lambda j: (0, 0, 0))) for e in errors],
             [(shape((1, 2, feats, model)), pl.BlockSpec((1, 2, tile, model), lambda j: (0, 0, j, 0)))],
-            grid=(feats // tile,),
+            scratch=[pltpu.VMEM((2, tokens, 2 * model), bf16)],
+            limit=46,
+            grid=(tiles,),
         )
         return out
 
@@ -613,27 +550,28 @@
             f(i)
 
     enter(0)
+    at(part, 1)
     summed(0)
     split_decoder()
-    at(part, 1)
-    goals()
     at(summed, 1)
-    for i in range(last + 1):
+    for i in range(last + 2):
+        if i:
+            at(summed, i + 1)
+        at(turn, i - 3)
         at(gate, i)
+        if i == 0:
+            goals()
+        at(across, i - 2)
+        at(held, i - 1)
         at(part, i + 2)
         at(recon, i)
-        at(across, i - 1)
-        at(summed, i + 2)
-        if i == last - 1:
-            at(finish, 0)
-        at(held, i)
-        at(back, i - 1)
-        at(middle, i)
-        at(turn, i - 1)
-        if i == last - 1:
-            at(finish, 1)
+        at(middle, i - 1)
+        at(back, i - 2)
+        if i >= last - 1:
+            at(finish, i - last + 1)
+    turn(last - 1)
     dec_grad = decoder_grad()
-    for i in range(2, last):
+    for i in range(3, last):
         finish(i)
     return dec_grad, saved["grad"]
 

time: 471 us -> 411 us (0.87)
  Pallas kernels: 234 us -> 173 us
  local copies, waits for them, and re-layouts: 16.7 us -> 27.9 us
  starting transfers between devices: 71.8 us -> 66.7 us
    pallas_call x63 -> x53, Pallas kernels: 234 us -> 173 us  [__call__(): pl.pallas_call(kernel, grid=grid or (), in_specs=in_specs, out_specs=[s f...]
    ppermute x6 -> x5, waiting for transfers between devices: 41.6 us -> 66.7 us  [middle(): lax.ppermute(value, 'feat', [(k, k ^ 2) for k in range(feat_size)])]
    ppermute x6 -> x5, waiting for transfers between devices: 20.1 us -> 0.01 us  [recon(): store[i]['in'] = lax.ppermute(r1, 'layer', [(0, 1)])]
    ppermute x6 -> x5, waiting for transfers between devices: 38.7 us -> 24.1 us  [across(): store[i]['in'] = lax.ppermute(value, 'layer', [(1, 0)])]
    ppermute x72 -> x60, waiting for transfers between devices: 17.1 us -> 3.46 us  [swap_near(): return [lax.ppermute(a, 'width', near_pairs) for a in arrays]]
    unnamed x78, local copies, waits for them, and re-layouts: 9.63 us -> 22.2 us
    ppermute x12 -> x10, waiting for transfers between devices: 11.7 us -> 24 us  [swap_far(): return lax.ppermute(a, 'width', far_pairs)]
    ppermute x6 -> x5, waiting for transfers between devices: 12.6 us -> 22.2 us  [held(): lax.ppermute(value, 'feat', [(k, k ^ 1) for k in range(feat_size)])]
  transfers between devices with their start and end apart: 109 -> 91, of which waited for: 55 -> 24; matrix products, arithmetic and copies ran while one was open for 1% -> 1% of each run, Pallas kernels for 47% -> 40%
where the time goes in v2:
time: 411 us; the launch traced here: 410 us
  Pallas kernels  173 us (42%)
  waiting for transfers between devices  141 us (34%)
  starting transfers between devices  66.7 us (16%)
  local copies, waits for them, and re-layouts  27.9 us (7%)
    pallas_call x53, Pallas kernels, __call__(): pl.pallas_call(kernel, grid=grid or (), in_specs=in_specs, out_specs=[s f...  173 us
    ppermute x5, waiting for transfers between devices, middle(): lax.ppermute(value, 'feat', [(k, k ^ 2) for k in range(feat_size)])  66.7 us
    ppermute x5, waiting for transfers between devices, across(): store[i]['in'] = lax.ppermute(value, 'layer', [(1, 0)])  24.1 us
    ppermute x10, waiting for transfers between devices, swap_far(): return lax.ppermute(a, 'width', far_pairs)  24 us
    ppermute x5, waiting for transfers between devices, held(): lax.ppermute(value, 'feat', [(k, k ^ 1) for k in range(feat_size)])  22.2 us
    unnamed x78, local copies, waits for them, and re-layouts  22.2 us
    ppermute x10, starting transfers between devices, swap_far(): return lax.ppermute(a, 'width', far_pairs)  14.6 us
    ppermute x60, starting transfers between devices, swap_near(): return [lax.ppermute(a, 'width', near_pairs) for a in arrays]  14.3 us
  transfers between devices with their start and end apart: 91, of which 24 were waited for; matrix products, arithmetic and copies ran while one was open for 1% of the time, Pallas kernels for 40%

profile of v2, /device:TPU:0, one launch (start us, length us, event | category | flops | bytes accessed | tf_op | source)
XLA Modules:
  0.0 410.4 jit_solution(14653150358798659949)
XLA Ops:
  2.6 8.5 %enter.1 = (f32[64,4096]{1,0:T(8,128)S(1)}, f32[16,4096]{1,0:T(8,128)S(1)}, f32[16,4096]{1,0:T(8,128)S(1)}, f32[16,4096]{1,0:T(8,128)S(1)}, f32[16,4096]{1,0:T(8...) custom-call(f32[128,512]{1,0:T(8,128)S(1)} %bitcast.65, ...), custom_call_target="tpu_custom_call" | custom-call | tf_op jit(solution)/shard_map/enter/pallas_call | solution.py:89
  15.0 4.0 part.4
  20.3 3.0 collective-permute-start.9
  23.3 8.4 %split_decoder.1 = (bf16[2,4096,512]{2,1,0:T(8,128)(2,1)S(1)}, bf16[2,4096,512]{2,1,0:T(8,128)(2,1)S(1)}, f32[8,128]{1,0:T(8,128)S(1)}) custom-call(f32[1,2,4096,512]{3,2,1,0:T(8,128)} %refs_0_.1, f32[8,128]{1,0:T(8,128)S(1)} %get-tuple-element.205.refs_1_), custom_call_target="tpu_custom_call" | custom-call | tf_op jit(solution)/shard_map/split_decoder/pallas_call | solution.py:89
  31.8 3.4 copy-done
  35.2 3.3 copy-done.2
  40.1 7.2 %collective-permute-done.9.refs_2_ = f32[64,4096]{1,0:T(8,128)S(1)} collective-permute-done((f32[64,4096]{1,0:T(8,128)S(1)}, f32[64,4096]{1,0:T(8,128)S(1)}, u32[]{:S(2)}, u32[]{:S(2)}) %collective-permute-start.9) | collective-permute-done | bytes 1048608 | tf_op jit(solution)/shard_map/ppermute | solution.py:139
  57.5 5.4 %part.5 = (f32[128,4096]{1,0:T(8,128)S(1)}, f32[32,4096]{1,0:T(8,128)}, f32[32,4096]{1,0:T(8,128)}, f32[32,4096]{1,0:T(8,128)}, f32[32,4096]{1,0:T(8,128)}, /*index=5*/f32[8,128]{1,0:T(8,128)S(1)}) custom-call(f32[256,512]{1,0:T(8,128)S(1)} %bitcast.63, bf16[512,4096]{1,0:T(8,128)(2,1)S(1)} %copy-done.5, bf16[512,4096]{1,0:T(8,128)(2,1)S(1)} %copy-done.8, ...), custom_call_target="tpu_custom_call" | custom-call | tf_op jit(solution)/shard_map/part/pallas_call | solution.py:89
  68.1 3.4 copy-done.1
  71.5 3.4 copy-done.3
  74.9 4.6 %recon.5 = (f32[128,512]{1,0:T(8,128)S(1)}, f32[128,512]{1,0:T(8,128)S(1)}, bf16[4,1024,4096]{2,1,0:T(8,128)(2,1)}, f32[8,128]{1,0:T(8,128)S(1)}) custom-call(f32[16,4096]{1,0:T(8,128)S(1)} %get-tuple-element.217.refs_0_, f32[16,4096]{1,0:T(8,128)S(1)} %get-tuple-element.218.refs_1_, f32[16,4096]{1,0:T(8,128)S(1)} %copy-done.16, f32[16,4096]{1,0:T(8,128)S(1)} %copy-done.18, ...), custom_call_target="tpu_custom_call" | custom-call | tf_op jit(solution)/shard_map/recon/pallas_call | solution.py:89
  79.6 2.3 collective-permute-start.22
  81.9 3.2 chip_sum.7
  87.2 5.1 %collective-permute-done.8.refs_2_ = f32[128,4096]{1,0:T(8,128)} collective-permute-done((f32[128,4096]{1,0:T(8,128)}, f32[128,4096]{1,0:T(8,128)}, u32[]{:S(2)}, u32[]{:S(2)}) %collective-permute-start.8) | collective-permute-done | bytes 2097184 | tf_op jit(solution)/shard_map/ppermute | solution.py:139
  92.3 3.3 gate.6
  99.0 4.6 %collective-permute-done.25.refs_1_ = f32[128,512]{1,0:T(8,128)S(1)} collective-permute-done((f32[128,512]{1,0:T(8,128)S(1)}, f32[128,512]{1,0:T(8,128)S(1)}, u32[]{:S(2)}, u32[]{:S(2)}) %collective-permute-start.25) | collective-permute-done | bytes 262176 | tf_op jit(solution)/shard_map/ppermute | solution.py:394
  103.6 4.1 part.6
  108.9 8.5 %recon.6 = (f32[256,512]{1,0:T(8,128)S(1)}, f32[256,512]{1,0:T(8,128)S(1)}, bf16[4,1024,4096]{2,1,0:T(8,128)(2,1)}, f32[8,128]{1,0:T(8,128)S(1)}) custom-call(f32[32,4096]{1,0:T(8,128)S(1)} %get-tuple-element.226.refs_0_, f32[32,4096]{1,0:T(8,128)S(1)} %get-tuple-element.227.refs_1_, ...), custom_call_target="tpu_custom_call", output_to_operand_aliasing={{2}: (10, {})} | custom-call | tf_op jit(solution)/shard_map/recon/pallas_call | solution.py:89
  117.5 3.4 collective-permute-start.24
  120.9 2.7 collective-permute-start.26
  125.6 11.7 %collective-permute-done.27.refs_2_ = f32[128,4096]{1,0:T(8,128)} collective-permute-done((f32[128,4096]{1,0:T(8,128)}, f32[128,4096]{1,0:T(8,128)}, u32[]{:S(2)}, u32[]{:S(2)}) %collective-permute-start.27) | collective-permute-done | bytes 2097184 | tf_op jit(solution)/shard_map/ppermute | solution.py:139
  137.3 3.1 gate.7
  141.8 2.2 collective-permute-start.37
  145.8 6.4 %collective-permute-done.36.refs_2_ = f32[128,512]{1,0:T(8,128)S(1)} collective-permute-done((f32[128,512]{1,0:T(8,128)S(1)}, f32[128,512]{1,0:T(8,128)S(1)}, u32[]{:S(2)}, u32[]{:S(2)}) %collective-permute-start.36) | collective-permute-done | bytes 262176 | tf_op jit(solution)/shard_map/ppermute | solution.py:431
  152.2 2.4 collective-permute-done.37.refs_1_
  154.7 2.4 part.7
  158.3 8.6 %recon.7 = (f32[256,512]{1,0:T(8,128)S(1)}, f32[256,512]{1,0:T(8,128)S(1)}, bf16[4,1024,4096]{2,1,0:T(8,128)(2,1)}, f32[8,128]{1,0:T(8,128)S(1)}) custom-call(f32[32,4096]{1,0:T(8,128)S(1)} %get-tuple-element.261.refs_0_, f32[32,4096]{1,0:T(8,128)S(1)} %get-tuple-element.262.refs_1_, ...), custom_call_target="tpu_custom_call", output_to_operand_aliasing={{2}: (10, {})} | custom-call | tf_op jit(solution)/shard_map/recon/pallas_call | solution.py:89
  167.0 9.2 %back.5 = (f32[64,4096]{1,0:T(8,128)S(1)}, f32[16,4096]{1,0:T(8,128)S(1)}, f32[16,4096]{1,0:T(8,128)S(1)}, f32[16,4096]{1,0:T(8,128)S(1)}, f32[16,4096]{1,0:T(8,...) custom-call(s32[2]{0:T(128)S(1)} %pad_add_fusion.refs_0_, f32[128,512]{1,0:T(8,128)S(1)} %get-tuple-element.259.refs_1_, ...), custom_call_target="tpu_custom_call" | custom-call | tf_op jit(solution)/shard_map/back/pallas_call | solution.py:89
  177.8 2.5 collective-permute-start.43
  180.4 3.5 collective-permute-start.50
  186.9 17.3 %collective-permute-done.43.refs_2_ = f32[256,512]{1,0:T(8,128)S(1)} collective-permute-done((f32[256,512]{1,0:T(8,128)S(1)}, f32[256,512]{1,0:T(8,128)S(1)}, u32[]{:S(2)}, u32[]{:S(2)}) %collective-permute-start.43) | collective-permute-done | bytes 524320 | tf_op jit(solution)/shard_map/ppermute | solution.py:414
  209.2 8.5 %recon.8 = (f32[256,512]{1,0:T(8,128)S(1)}, f32[256,512]{1,0:T(8,128)S(1)}, bf16[4,1024,4096]{2,1,0:T(8,128)(2,1)}, f32[8,128]{1,0:T(8,128)S(1)}) custom-call(f32[32,4096]{1,0:T(8,128)S(1)} %get-tuple-element.286.refs_0_, f32[32,4096]{1,0:T(8,128)S(1)} %get-tuple-element.287.refs_1_, ...), custom_call_target="tpu_custom_call", output_to_operand_aliasing={{2}: (10, {})} | custom-call | tf_op jit(solution)/shard_map/recon/pallas_call | solution.py:89
  222.1 8.0 %back.6 = (f32[128,4096]{1,0:T(8,128)S(1)}, f32[32,4096]{1,0:T(8,128)S(1)}, f32[32,4096]{1,0:T(8,128)S(1)}, f32[32,4096]{1,0:T(8,128)S(1)}, f32[32,4096]{1,0:T(8...) custom-call(s32[2]{0:T(128)S(1)} %pad_add_fusion.refs_0_, f32[256,512]{1,0:T(8,128)S(1)} %get-tuple-element.281.refs_1_, ...), custom_call_target="tpu_custom_call" | custom-call | tf_op jit(solution)/shard_map/back/pallas_call | solution.py:89
  232.1 3.4 collective-permute-start.65
  239.0 19.9 %collective-permute-done.65.refs_2_ = f32[256,512]{1,0:T(8,128)S(1)} collective-permute-done((f32[256,512]{1,0:T(8,128)S(1)}, f32[256,512]{1,0:T(8,128)S(1)}, u32[]{:S(2)}, u32[]{:S(2)}) %collective-permute-start.65) | collective-permute-done | bytes 524320 | tf_op jit(solution)/shard_map/ppermute | solution.py:414
  263.8 4.7 %recon.9 = (f32[128,512]{1,0:T(8,128)S(1)}, f32[128,512]{1,0:T(8,128)S(1)}, bf16[4,1024,4096]{2,1,0:T(8,128)(2,1)}, f32[8,128]{1,0:T(8,128)S(1)}) custom-call(f32[16,4096]{1,0:T(8,128)S(1)} %get-tuple-element.301.refs_0_, f32[16,4096]{1,0:T(8,128)S(1)} %get-tuple-element.302.refs_1_, ...), custom_call_target="tpu_custom_call", output_to_operand_aliasing={{2}: (10, {})} | custom-call | tf_op jit(solution)/shard_map/recon/pallas_call | solution.py:89
  268.5 5.5 %collective-permute-done.67.refs_1_ = f32[256,512]{1,0:T(8,128)S(1)} collective-permute-done((f32[256,512]{1,0:T(8,128)S(1)}, f32[256,512]{1,0:T(8,128)S(1)}, u32[]{:S(2)}, u32[]{:S(2)}) %collective-permute-start.67) | collective-permute-done | bytes 524320 | tf_op jit(solution)/shard_map/ppermute | solution.py:394
  274.0 2.5 collective-permute-done.66.refs_2_
  276.5 8.0 %back.7 = (f32[128,4096]{1,0:T(8,128)S(1)}, f32[32,4096]{1,0:T(8,128)S(1)}, f32[32,4096]{1,0:T(8,128)S(1)}, f32[32,4096]{1,0:T(8,128)S(1)}, f32[32,4096]{1,0:T(8...) custom-call(s32[2]{0:T(128)S(1)} %pad_add_fusion.refs_0_, f32[256,512]{1,0:T(8,128)S(1)} %get-tuple-element.315.refs_1_, ...), custom_call_target="tpu_custom_call" | custom-call | tf_op jit(solution)/shard_map/back/pallas_call | solution.py:89
  285.7 2.9 collective-permute-start.68
  293.2 18.7 %collective-permute-done.68.refs_2_ = f32[256,512]{1,0:T(8,128)S(1)} collective-permute-done((f32[256,512]{1,0:T(8,128)S(1)}, f32[256,512]{1,0:T(8,128)S(1)}, u32[]{:S(2)}, u32[]{:S(2)}) %collective-permute-start.68) | collective-permute-done | bytes 524320 | tf_op jit(solution)/shard_map/ppermute | solution.py:414
  314.6 7.7 %collective-permute-done.76.refs_1_ = f32[128,512]{1,0:T(8,128)S(1)} collective-permute-done((f32[128,512]{1,0:T(8,128)S(1)}, f32[128,512]{1,0:T(8,128)S(1)}, u32[]{:S(2)}, u32[]{:S(2)}) %collective-permute-start.76) | collective-permute-done | bytes 262176 | tf_op jit(solution)/shard_map/ppermute | solution.py:394
  322.3 5.4 %collective-permute-done.74.refs_2_ = f32[256,512]{1,0:T(8,128)S(1)} collective-permute-done((f32[256,512]{1,0:T(8,128)S(1)}, f32[256,512]{1,0:T(8,128)S(1)}, u32[]{:S(2)}, u32[]{:S(2)}) %collective-permute-start.74) | collective-permute-done | bytes 524320 | tf_op jit(solution)/shard_map/ppermute | solution.py:431
  327.8 8.0 %back.8 = (f32[128,4096]{1,0:T(8,128)S(1)}, f32[32,4096]{1,0:T(8,128)S(1)}, f32[32,4096]{1,0:T(8,128)S(1)}, f32[32,4096]{1,0:T(8,128)S(1)}, f32[32,4096]{1,0:T(8...) custom-call(s32[2]{0:T(128)S(1)} %pad_add_fusion.refs_0_, f32[256,512]{1,0:T(8,128)S(1)} %get-tuple-element.332.refs_1_, ...), custom_call_target="tpu_custom_call" | custom-call | tf_op jit(solution)/shard_map/back/pallas_call | solution.py:89
  341.7 10.8 %collective-permute-done.77.refs_2_ = f32[128,512]{1,0:T(8,128)S(1)} collective-permute-done((f32[128,512]{1,0:T(8,128)S(1)}, f32[128,512]{1,0:T(8,128)S(1)}, u32[]{:S(2)}, u32[]{:S(2)}) %collective-permute-start.77) | collective-permute-done | bytes 262176 | tf_op jit(solution)/shard_map/ppermute | solution.py:414
  355.6 7.6 %collective-permute-done.83.refs_2_ = f32[128,512]{1,0:T(8,128)S(1)} collective-permute-done((f32[128,512]{1,0:T(8,128)S(1)}, f32[128,512]{1,0:T(8,128)S(1)}, u32[]{:S(2)}, u32[]{:S(2)}) %collective-permute-start.83) | collective-permute-done | bytes 262176 | tf_op jit(solution)/shard_map/ppermute | solution.py:431
  363.2 9.2 %back.9 = (f32[64,4096]{1,0:T(8,128)S(1)}, f32[16,4096]{1,0:T(8,128)S(1)}, f32[16,4096]{1,0:T(8,128)S(1)}, f32[16,4096]{1,0:T(8,128)S(1)}, f32[16,4096]{1,0:T(8,...) custom-call(s32[2]{0:T(128)S(1)} %pad_add_fusion.refs_0_, f32[128,512]{1,0:T(8,128)S(1)} %get-tuple-element.353.refs_1_, ...), custom_call_target="tpu_custom_call" | custom-call | tf_op jit(solution)/shard_map/back/pallas_call | solution.py:89
  376.8 30.8 %decoder_grad.1 = (f32[1,2,4096,512]{3,2,1,0:T(8,128)}, f32[8,128]{1,0:T(8,128)S(1)}) custom-call(bf16[4,1024,4096]{2,1,0:T(8,128)(2,1)} %get-tuple-element.312.refs_0_, bf16[2,128,1024]{2,1,0:T(8,128)(2,1)S(1)} %get-tuple-element.313.refs_1_, bf16[2,256,1024]{2,1,0:T(8,128)(2,1)S(1)} %get-tuple-element.314.refs_2_, ...), custom_call_target="tpu_custom_call" | custom-call | tf_op jit(solution)/shard_map/decoder_grad/pallas_call | solution.py:89
  (293 shorter events, 85.8 us)
Async XLA Ops:
  19.1 19.4 %collective-permute-start = (f32[32,4096]{1,0:T(8,128)S(1)}, f32[32,4096]{1,0:T(8,128)S(1)}, u32[]{:S(2)}, u32[]{:S(2)}) collective-permute-start(f32[32,4096]{1,0:T(8,128)S(1)} %get-tuple-element.195), channel_id=1, source_target_pairs={{0,1},{1,0},{2,3},{3,2},{4,5},{5,4},{6,7},{7,6},{8,9},{9,8},{10,11... | collective-permute-start | bytes 1572872 | tf_op jit(solution)/shard_map/ppermute | solution.py:136
  19.6 18.8 %collective-permute-start.1 = (f32[32,4096]{1,0:T(8,128)S(1)}, f32[32,4096]{1,0:T(8,128)S(1)}, u32[]{:S(2)}, u32[]{:S(2)}) collective-permute-start(f32[32,4096]{1,0:T(8,128)S(1)} %get-tuple-element.196), channel_id=1, source_target_pairs={{0,1},{1,0},{2,3},{3,2},{4,5},{5,4},{6,7},{7,6},{8,9},{9,8},{10,11... | collective-permute-start | bytes 1572872 | tf_op jit(solution)/shard_map/ppermute | solution.py:136
  19.7 18.7 %collective-permute-start.2 = (f32[32,4096]{1,0:T(8,128)S(1)}, f32[32,4096]{1,0:T(8,128)S(1)}, u32[]{:S(2)}, u32[]{:S(2)}) collective-permute-start(f32[32,4096]{1,0:T(8,128)S(1)} %get-tuple-element.197), channel_id=1, source_target_pairs={{0,1},{1,0},{2,3},{3,2},{4,5},{5,4},{6,7},{7,6},{8,9},{9,8},{10,11... | collective-permute-start | bytes 1572872 | tf_op jit(solution)/shard_map/ppermute | solution.py:136
  20.1 18.3 %collective-permute-start.3 = (f32[32,4096]{1,0:T(8,128)S(1)}, f32[32,4096]{1,0:T(8,128)S(1)}, u32[]{:S(2)}, u32[]{:S(2)}) collective-permute-start(f32[32,4096]{1,0:T(8,128)S(1)} %get-tuple-element.198), channel_id=1, source_target_pairs={{0,1},{1,0},{2,3},{3,2},{4,5},{5,4},{6,7},{7,6},{8,9},{9,8},{10,11... | collective-permute-start | bytes 1572872 | tf_op jit(solution)/shard_map/ppermute | solution.py:136
  20.3 26.9 %collective-permute-start.9 = (f32[64,4096]{1,0:T(8,128)S(1)}, f32[64,4096]{1,0:T(8,128)S(1)}, u32[]{:S(2)}, u32[]{:S(2)}) collective-permute-start(f32[64,4096]{1,0:T(8,128)S(1)} %get-tuple-element.208.refs_1_), channel_id=1, source_target_pairs={{0,2},{1,3},{2,0},{3,1},{4,6},{5,7},{6,4},{7,5},{8,10},{9,11},{10,... | collective-permute-start | bytes 3145736 | tf_op jit(solution)/shard_map/ppermute | solution.py:139
  40.0 52.3 %collective-permute-start.8 = (f32[128,4096]{1,0:T(8,128)}, f32[128,4096]{1,0:T(8,128)}, u32[]{:S(2)}, u32[]{:S(2)}) collective-permute-start(f32[128,4096]{1,0:T(8,128)} %get-tuple-element.207.refs_1_), channel_id=1, source_target_pairs={{0,2},{1,3},{2,0},{3,1},{4,6},{5,7},{6,4},{7,5},{8,10},{9,11},{10,... | collective-permute-start | bytes 6291464 | tf_op jit(solution)/shard_map/ppermute | solution.py:139
  48.4 14.5 %collective-permute-start.15 = (f32[16,4096]{1,0:T(8,128)S(1)}, f32[16,4096]{1,0:T(8,128)S(1)}, u32[]{:S(2)}, u32[]{:S(2)}) collective-permute-start(f32[16,4096]{1,0:T(8,128)S(1)} %get-tuple-element.218.refs_1_), channel_id=1, source_target_pairs={{0,1},{1,0},{2,3},{3,2},{4,5},{5,4},{6,7},{7,6},{8,9},{9,8},{10,11... | collective-permute-start | bytes 786440 | tf_op jit(solution)/shard_map/ppermute | solution.py:136
  48.9 14.8 %collective-permute-start.16 = (f32[16,4096]{1,0:T(8,128)S(1)}, f32[16,4096]{1,0:T(8,128)S(1)}, u32[]{:S(2)}, u32[]{:S(2)}) collective-permute-start(f32[16,4096]{1,0:T(8,128)S(1)} %get-tuple-element.219.refs_2_), channel_id=1, source_target_pairs={{0,1},{1,0},{2,3},{3,2},{4,5},{5,4},{6,7},{7,6},{8,9},{9,8},{10,11... | collective-permute-start | bytes 786440 | tf_op jit(solution)/shard_map/ppermute | solution.py:136
  49.0 15.9 %collective-permute-start.17 = (f32[16,4096]{1,0:T(8,128)S(1)}, f32[16,4096]{1,0:T(8,128)S(1)}, u32[]{:S(2)}, u32[]{:S(2)}) collective-permute-start(f32[16,4096]{1,0:T(8,128)S(1)} %get-tuple-element.220.refs_3_), channel_id=1, source_target_pairs={{0,1},{1,0},{2,3},{3,2},{4,5},{5,4},{6,7},{7,6},{8,9},{9,8},{10,11... | collective-permute-start | bytes 786440 | tf_op jit(solution)/shard_map/ppermute | solution.py:136
  51.1 14.5 %collective-permute-start.23 = (f32[128,512]{1,0:T(8,128)S(1)}, f32[128,512]{1,0:T(8,128)S(1)}, u32[]{:S(2)}, u32[]{:S(2)}) collective-permute-start(f32[128,512]{1,0:T(8,128)S(1)} %get-tuple-element.234), channel_id=1, source_target_pairs={{0,16},{16,0},{1,17},{17,1},{2,18},{18,2},{3,19},{19,3},{4,20},{20... | collective-permute-start | bytes 786440 | tf_op jit(solution)/shard_map/ppermute | solution.py:290
  63.7 15.9 %collective-permute-start.10 = (f32[32,4096]{1,0:T(8,128)}, f32[32,4096]{1,0:T(8,128)}, u32[]{:S(2)}, u32[]{:S(2)}) collective-permute-start(f32[32,4096]{1,0:T(8,128)} %get-tuple-element.213), channel_id=1, source_target_pairs={{0,1},{1,0},{2,3},{3,2},{4,5},{5,4},{6,7},{7,6},{8,9},{9,8},{10,11... | collective-permute-start | bytes 1572872 | tf_op jit(solution)/shard_map/ppermute | solution.py:136
  64.4 17.5 %collective-permute-start.11 = (f32[32,4096]{1,0:T(8,128)}, f32[32,4096]{1,0:T(8,128)}, u32[]{:S(2)}, u32[]{:S(2)}) collective-permute-start(f32[32,4096]{1,0:T(8,128)} %get-tuple-element.214), channel_id=1, source_target_pairs={{0,1},{1,0},{2,3},{3,2},{4,5},{5,4},{6,7},{7,6},{8,9},{9,8},{10,11... | collective-permute-start | bytes 1572872 | tf_op jit(solution)/shard_map/ppermute | solution.py:136
  65.6 16.3 %collective-permute-start.12 = (f32[32,4096]{1,0:T(8,128)}, f32[32,4096]{1,0:T(8,128)}, u32[]{:S(2)}, u32[]{:S(2)}) collective-permute-start(f32[32,4096]{1,0:T(8,128)} %get-tuple-element.215), channel_id=1, source_target_pairs={{0,1},{1,0},{2,3},{3,2},{4,5},{5,4},{6,7},{7,6},{8,9},{9,8},{10,11... | collective-permute-start | bytes 1572872 | tf_op jit(solution)/shard_map/ppermute | solution.py:136
  66.3 15.6 %collective-permute-start.13 = (f32[32,4096]{1,0:T(8,128)}, f32[32,4096]{1,0:T(8,128)}, u32[]{:S(2)}, u32[]{:S(2)}) collective-permute-start(f32[32,4096]{1,0:T(8,128)} %get-tuple-element.216), channel_id=1, source_target_pairs={{0,1},{1,0},{2,3},{3,2},{4,5},{5,4},{6,7},{7,6},{8,9},{9,8},{10,11... | collective-permute-start | bytes 1572872 | tf_op jit(solution)/shard_map/ppermute | solution.py:136
  79.6 16.0 %collective-permute-start.22 = (f32[128,512]{1,0:T(8,128)S(1)}, f32[128,512]{1,0:T(8,128)S(1)}, u32[]{:S(2)}, u32[]{:S(2)}) collective-permute-start(f32[128,512]{1,0:T(8,128)S(1)} %get-tuple-element.232.refs_2_), channel_id=1, source_target_pairs={{0,16},{1,17},{2,18},{3,19},{4,20},{5,21},{6,22},{7,23},{8,24},{9,... | collective-permute-start | bytes 786440 | tf_op jit(solution)/shard_map/ppermute | solution.py:376
  85.1 52.1 %collective-permute-start.27 = (f32[128,4096]{1,0:T(8,128)}, f32[128,4096]{1,0:T(8,128)}, u32[]{:S(2)}, u32[]{:S(2)}) collective-permute-start(f32[128,4096]{1,0:T(8,128)} %get-tuple-element.243.refs_1_), channel_id=1, source_target_pairs={{0,2},{1,3},{2,0},{3,1},{4,6},{5,7},{6,4},{7,5},{8,10},{9,11},{10,... | collective-permute-start | bytes 6291464 | tf_op jit(solution)/shard_map/ppermute | solution.py:139
  108.4 15.2 %collective-permute-start.30 = (f32[32,4096]{1,0:T(8,128)S(1)}, f32[32,4096]{1,0:T(8,128)S(1)}, u32[]{:S(2)}, u32[]{:S(2)}) collective-permute-start(f32[32,4096]{1,0:T(8,128)S(1)} %get-tuple-element.247), channel_id=1, source_target_pairs={{0,1},{1,0},{2,3},{3,2},{4,5},{5,4},{6,7},{7,6},{8,9},{9,8},{10,11... | collective-permute-start | bytes 1572872 | tf_op jit(solution)/shard_map/ppermute | solution.py:136
  108.8 14.7 %collective-permute-start.31 = (f32[32,4096]{1,0:T(8,128)S(1)}, f32[32,4096]{1,0:T(8,128)S(1)}, u32[]{:S(2)}, u32[]{:S(2)}) collective-permute-start(f32[32,4096]{1,0:T(8,128)S(1)} %get-tuple-element.248), channel_id=1, source_target_pairs={{0,1},{1,0},{2,3},{3,2},{4,5},{5,4},{6,7},{7,6},{8,9},{9,8},{10,11... | collective-permute-start | bytes 1572872 | tf_op jit(solution)/shard_map/ppermute | solution.py:136
  117.5 23.5 %collective-permute-start.24 = (f32[256,512]{1,0:T(8,128)S(1)}, f32[256,512]{1,0:T(8,128)S(1)}, u32[]{:S(2)}, u32[]{:S(2)}) collective-permute-start(f32[256,512]{1,0:T(8,128)S(1)} %get-tuple-element.239.refs_2_), channel_id=1, source_target_pairs={{0,16},{1,17},{2,18},{3,19},{4,20},{5,21},{6,22},{7,23},{8,24},{9,... | collective-permute-start | bytes 1572872 | tf_op jit(solution)/shard_map/ppermute | solution.py:376
  120.9 19.5 %collective-permute-start.26 = (f32[128,512]{1,0:T(8,128)S(1)}, f32[128,512]{1,0:T(8,128)S(1)}, u32[]{:S(2)}, u32[]{:S(2)}) collective-permute-start(f32[128,512]{1,0:T(8,128)S(1)} %get-tuple-element.242.refs_1_), channel_id=1, source_target_pairs={{0,8},{4,12},{8,0},{12,4},{1,9},{5,13},{9,1},{13,5},{2,10},{6,14},... | collective-permute-start | bytes 786440 | tf_op jit(solution)/shard_map/ppermute | solution.py:414
  123.8 60.8 %collective-permute-start.44 = (f32[128,4096]{1,0:T(8,128)S(1)}, f32[128,4096]{1,0:T(8,128)S(1)}, u32[]{:S(2)}, u32[]{:S(2)}) collective-permute-start(f32[128,4096]{1,0:T(8,128)S(1)} %get-tuple-element.272.refs_1_), channel_id=1, source_target_pairs={{0,2},{1,3},{2,0},{3,1},{4,6},{5,7},{6,4},{7,5},{8,10},{9,11},{10,... | collective-permute-start | bytes 6291464 | tf_op jit(solution)/shard_map/ppermute | solution.py:139
  141.8 12.9 %collective-permute-start.37 = (f32[256,512]{1,0:T(8,128)S(1)}, f32[256,512]{1,0:T(8,128)S(1)}, u32[]{:S(2)}, u32[]{:S(2)}) collective-permute-start(f32[256,512]{1,0:T(8,128)S(1)} %get-tuple-element.260.refs_0_), channel_id=1, source_target_pairs={{0,4},{4,0},{8,12},{12,8},{1,5},{5,1},{9,13},{13,9},{2,6},{6,2},{1... | collective-permute-start | bytes 1572872 | tf_op jit(solution)/shard_map/ppermute | solution.py:394
  157.2 19.0 %collective-permute-start.32 = (f32[16,4096]{1,0:T(8,128)S(1)}, f32[16,4096]{1,0:T(8,128)S(1)}, u32[]{:S(2)}, u32[]{:S(2)}) collective-permute-start(f32[16,4096]{1,0:T(8,128)S(1)} %get-tuple-element.255), channel_id=1, source_target_pairs={{0,1},{1,0},{2,3},{3,2},{4,5},{5,4},{6,7},{7,6},{8,9},{9,8},{10,11... | collective-permute-start | bytes 786440 | tf_op jit(solution)/shard_map/ppermute | solution.py:136
  157.7 19.0 %collective-permute-start.33 = (f32[16,4096]{1,0:T(8,128)S(1)}, f32[16,4096]{1,0:T(8,128)S(1)}, u32[]{:S(2)}, u32[]{:S(2)}) collective-permute-start(f32[16,4096]{1,0:T(8,128)S(1)} %get-tuple-element.256), channel_id=1, source_target_pairs={{0,1},{1,0},{2,3},{3,2},{4,5},{5,4},{6,7},{7,6},{8,9},{9,8},{10,11... | collective-permute-start | bytes 786440 | tf_op jit(solution)/shard_map/ppermute | solution.py:136
  157.8 19.0 %collective-permute-start.34 = (f32[16,4096]{1,0:T(8,128)S(1)}, f32[16,4096]{1,0:T(8,128)S(1)}, u32[]{:S(2)}, u32[]{:S(2)}) collective-permute-start(f32[16,4096]{1,0:T(8,128)S(1)} %get-tuple-element.257), channel_id=1, source_target_pairs={{0,1},{1,0},{2,3},{3,2},{4,5},{5,4},{6,7},{7,6},{8,9},{9,8},{10,11... | collective-permute-start | bytes 786440 | tf_op jit(solution)/shard_map/ppermute | solution.py:136
  158.2 19.0 %collective-permute-start.35 = (f32[16,4096]{1,0:T(8,128)S(1)}, f32[16,4096]{1,0:T(8,128)S(1)}, u32[]{:S(2)}, u32[]{:S(2)}) collective-permute-start(f32[16,4096]{1,0:T(8,128)S(1)} %get-tuple-element.258), channel_id=1, source_target_pairs={{0,1},{1,0},{2,3},{3,2},{4,5},{5,4},{6,7},{7,6},{8,9},{9,8},{10,11... | collective-permute-start | bytes 786440 | tf_op jit(solution)/shard_map/ppermute | solution.py:136
  177.8 26.3 %collective-permute-start.43 = (f32[256,512]{1,0:T(8,128)S(1)}, f32[256,512]{1,0:T(8,128)S(1)}, u32[]{:S(2)}, u32[]{:S(2)}) collective-permute-start(f32[256,512]{1,0:T(8,128)S(1)} %get-tuple-element.271.refs_1_), channel_id=1, source_target_pairs={{0,8},{4,12},{8,0},{12,4},{1,9},{5,13},{9,1},{13,5},{2,10},{6,14},... | collective-permute-start | bytes 1572872 | tf_op jit(solution)/shard_map/ppermute | solution.py:414
  180.4 24.4 %collective-permute-start.50 = (f32[256,512]{1,0:T(8,128)S(1)}, f32[256,512]{1,0:T(8,128)S(1)}, u32[]{:S(2)}, u32[]{:S(2)}) collective-permute-start(f32[256,512]{1,0:T(8,128)S(1)} %get-tuple-element.283.refs_2_), channel_id=1, source_target_pairs={{0,16},{1,17},{2,18},{3,19},{4,20},{5,21},{6,22},{7,23},{8,24},{9,... | collective-permute-start | bytes 1572872 | tf_op jit(solution)/shard_map/ppermute | solution.py:376
  186.0 20.1 %collective-permute-start.52 = (f32[32,4096]{1,0:T(8,128)S(1)}, f32[32,4096]{1,0:T(8,128)S(1)}, u32[]{:S(2)}, u32[]{:S(2)}) collective-permute-start(f32[32,4096]{1,0:T(8,128)S(1)} %get-tuple-element.286.refs_0_), channel_id=1, source_target_pairs={{0,1},{1,0},{2,3},{3,2},{4,5},{5,4},{6,7},{7,6},{8,9},{9,8},{10,11... | collective-permute-start | bytes 1572872 | tf_op jit(solution)/shard_map/ppermute | solution.py:136
  186.2 21.4 %collective-permute-start.53 = (f32[32,4096]{1,0:T(8,128)S(1)}, f32[32,4096]{1,0:T(8,128)S(1)}, u32[]{:S(2)}, u32[]{:S(2)}) collective-permute-start(f32[32,4096]{1,0:T(8,128)S(1)} %get-tuple-element.287.refs_1_), channel_id=1, source_target_pairs={{0,1},{1,0},{2,3},{3,2},{4,5},{5,4},{6,7},{7,6},{8,9},{9,8},{10,11... | collective-permute-start | bytes 1572872 | tf_op jit(solution)/shard_map/ppermute | solution.py:136
  186.8 22.5 %collective-permute-start.54 = (f32[32,4096]{1,0:T(8,128)S(1)}, f32[32,4096]{1,0:T(8,128)S(1)}, u32[]{:S(2)}, u32[]{:S(2)}) collective-permute-start(f32[32,4096]{1,0:T(8,128)S(1)} %get-tuple-element.288.refs_2_), channel_id=1, source_target_pairs={{0,1},{1,0},{2,3},{3,2},{4,5},{5,4},{6,7},{7,6},{8,9},{9,8},{10,11... | collective-permute-start | bytes 1572872 | tf_op jit(solution)/shard_map/ppermute | solution.py:136
  205.4 14.4 %collective-permute-start.51 = (f32[256,512]{1,0:T(8,128)S(1)}, f32[256,512]{1,0:T(8,128)S(1)}, u32[]{:S(2)}, u32[]{:S(2)}) collective-permute-start(f32[256,512]{1,0:T(8,128)S(1)} %get-tuple-element.285.refs_0_), channel_id=1, source_target_pairs={{0,4},{4,0},{8,12},{12,8},{1,5},{5,1},{9,13},{13,9},{2,6},{6,2},{1... | collective-permute-start | bytes 1572872 | tf_op jit(solution)/shard_map/ppermute | solution.py:394
  206.1 15.9 %collective-permute-start.49 = (f32[256,512]{1,0:T(8,128)S(1)}, f32[256,512]{1,0:T(8,128)S(1)}, u32[]{:S(2)}, u32[]{:S(2)}) collective-permute-start(f32[256,512]{1,0:T(8,128)S(1)} %get-tuple-element.281.refs_1_), channel_id=1, source_target_pairs={{16,0},{17,1},{18,2},{19,3},{20,4},{21,5},{22,6},{23,7},{24,8},{25... | collective-permute-start | bytes 1572872 | tf_op jit(solution)/shard_map/ppermute | solution.py:431
  207.7 30.2 %collective-permute-start.42 = (f32[64,4096]{1,0:T(8,128)S(1)}, f32[64,4096]{1,0:T(8,128)S(1)}, u32[]{:S(2)}, u32[]{:S(2)}) collective-permute-start(f32[64,4096]{1,0:T(8,128)S(1)} %get-tuple-element.270.refs_1_), channel_id=1, source_target_pairs={{0,2},{1,3},{2,0},{3,1},{4,6},{5,7},{6,4},{7,5},{8,10},{9,11},{10,... | collective-permute-start | bytes 3145736 | tf_op jit(solution)/shard_map/ppermute | solution.py:139
  232.1 26.8 %collective-permute-start.65 = (f32[256,512]{1,0:T(8,128)S(1)}, f32[256,512]{1,0:T(8,128)S(1)}, u32[]{:S(2)}, u32[]{:S(2)}) collective-permute-start(f32[256,512]{1,0:T(8,128)S(1)} %get-tuple-element.308.refs_1_), channel_id=1, source_target_pairs={{0,8},{4,12},{8,0},{12,4},{1,9},{5,13},{9,1},{13,5},{2,10},{6,14},... | collective-permute-start | bytes 1572872 | tf_op jit(solution)/shard_map/ppermute | solution.py:414
  235.4 24.1 %collective-permute-start.64 = (f32[256,512]{1,0:T(8,128)S(1)}, f32[256,512]{1,0:T(8,128)S(1)}, u32[]{:S(2)}, u32[]{:S(2)}) collective-permute-start(f32[256,512]{1,0:T(8,128)S(1)} %get-tuple-element.307.refs_2_), channel_id=1, source_target_pairs={{0,16},{1,17},{2,18},{3,19},{4,20},{5,21},{6,22},{7,23},{8,24},{9,... | collective-permute-start | bytes 1572872 | tf_op jit(solution)/shard_map/ppermute | solution.py:376
  238.9 23.3 %collective-permute-start.60 = (f32[16,4096]{1,0:T(8,128)S(1)}, f32[16,4096]{1,0:T(8,128)S(1)}, u32[]{:S(2)}, u32[]{:S(2)}) collective-permute-start(f32[16,4096]{1,0:T(8,128)S(1)} %get-tuple-element.301.refs_0_), channel_id=1, source_target_pairs={{0,1},{1,0},{2,3},{3,2},{4,5},{5,4},{6,7},{7,6},{8,9},{9,8},{10,11... | collective-permute-start | bytes 786440 | tf_op jit(solution)/shard_map/ppermute | solution.py:136
  260.2 13.8 %collective-permute-start.67 = (f32[256,512]{1,0:T(8,128)S(1)}, f32[256,512]{1,0:T(8,128)S(1)}, u32[]{:S(2)}, u32[]{:S(2)}) collective-permute-start(f32[256,512]{1,0:T(8,128)S(1)} %get-tuple-element.316.refs_0_), channel_id=1, source_target_pairs={{0,4},{4,0},{8,12},{12,8},{1,5},{5,1},{9,13},{13,9},{2,6},{6,2},{1... | collective-permute-start | bytes 1572872 | tf_op jit(solution)/shard_map/ppermute | solution.py:394
  260.3 16.2 %collective-permute-start.66 = (f32[256,512]{1,0:T(8,128)S(1)}, f32[256,512]{1,0:T(8,128)S(1)}, u32[]{:S(2)}, u32[]{:S(2)}) collective-permute-start(f32[256,512]{1,0:T(8,128)S(1)} %get-tuple-element.315.refs_1_), channel_id=1, source_target_pairs={{16,0},{17,1},{18,2},{19,3},{20,4},{21,5},{22,6},{23,7},{24,8},{25... | collective-permute-start | bytes 1572872 | tf_op jit(solution)/shard_map/ppermute | solution.py:431
  262.3 23.4 %collective-permute-start.73 = (f32[32,4096]{1,0:T(8,128)S(1)}, f32[32,4096]{1,0:T(8,128)S(1)}, u32[]{:S(2)}, u32[]{:S(2)}) collective-permute-start(f32[32,4096]{1,0:T(8,128)S(1)} %get-tuple-element.327), channel_id=1, source_target_pairs={{0,2},{1,3},{2,0},{3,1},{4,6},{5,7},{6,4},{7,5},{8,10},{9,11},{10,... | collective-permute-start | bytes 1572872 | tf_op jit(solution)/shard_map/ppermute | solution.py:139
  285.7 26.3 %collective-permute-start.68 = (f32[256,512]{1,0:T(8,128)S(1)}, f32[256,512]{1,0:T(8,128)S(1)}, u32[]{:S(2)}, u32[]{:S(2)}) collective-permute-start(f32[256,512]{1,0:T(8,128)S(1)} %get-tuple-element.320.refs_1_), channel_id=1, source_target_pairs={{0,8},{4,12},{8,0},{12,4},{1,9},{5,13},{9,1},{13,5},{2,10},{6,14},... | collective-permute-start | bytes 1572872 | tf_op jit(solution)/shard_map/ppermute | solution.py:414
  288.5 49.4 %collective-permute-start.82 = (f32[64,4096]{1,0:T(8,128)S(1)}, f32[64,4096]{1,0:T(8,128)S(1)}, u32[]{:S(2)}, u32[]{:S(2)}) collective-permute-start(f32[64,4096]{1,0:T(8,128)S(1)} %get-tuple-element.347), channel_id=1, source_target_pairs={{0,2},{1,3},{2,0},{3,1},{4,6},{5,7},{6,4},{7,5},{8,10},{9,11},{10,... | collective-permute-start | bytes 3145736 | tf_op jit(solution)/shard_map/ppermute | solution.py:139
  290.9 23.0 %collective-permute-start.75 = (f32[128,512]{1,0:T(8,128)S(1)}, f32[128,512]{1,0:T(8,128)S(1)}, u32[]{:S(2)}, u32[]{:S(2)}) collective-permute-start(f32[128,512]{1,0:T(8,128)S(1)} %get-tuple-element.334.refs_2_), channel_id=1, source_target_pairs={{0,16},{1,17},{2,18},{3,19},{4,20},{5,21},{6,22},{7,23},{8,24},{9,... | collective-permute-start | bytes 786440 | tf_op jit(solution)/shard_map/ppermute | solution.py:376
  312.5 15.2 %collective-permute-start.74 = (f32[256,512]{1,0:T(8,128)S(1)}, f32[256,512]{1,0:T(8,128)S(1)}, u32[]{:S(2)}, u32[]{:S(2)}) collective-permute-start(f32[256,512]{1,0:T(8,128)S(1)} %get-tuple-element.332.refs_1_), channel_id=1, source_target_pairs={{16,0},{17,1},{18,2},{19,3},{20,4},{21,5},{22,6},{23,7},{24,8},{25... | collective-permute-start | bytes 1572872 | tf_op jit(solution)/shard_map/ppermute | solution.py:431
  335.9 37.2 %collective-permute-start.88 = (f32[64,4096]{1,0:T(8,128)S(1)}, f32[64,4096]{1,0:T(8,128)S(1)}, u32[]{:S(2)}, u32[]{:S(2)}) collective-permute-start(f32[64,4096]{1,0:T(8,128)S(1)} %get-tuple-element.362), channel_id=1, source_target_pairs={{0,2},{1,3},{2,0},{3,1},{4,6},{5,7},{6,4},{7,5},{8,10},{9,11},{10,... | collective-permute-start | bytes 3145736 | tf_op jit(solution)/shard_map/ppermute | solution.py:139
  338.1 14.3 %collective-permute-start.77 = (f32[128,512]{1,0:T(8,128)S(1)}, f32[128,512]{1,0:T(8,128)S(1)}, u32[]{:S(2)}, u32[]{:S(2)}) collective-permute-start(f32[128,512]{1,0:T(8,128)S(1)} %get-tuple-element.340.refs_1_), channel_id=1, source_target_pairs={{0,8},{4,12},{8,0},{12,4},{1,9},{5,13},{9,1},{13,5},{2,10},{6,14},... | collective-permute-start | bytes 786440 | tf_op jit(solution)/shard_map/ppermute | solution.py:414
  354.6 53.0 %collective-permute-start.90 = (f32[64,4096]{1,0:T(8,128)S(1)}, f32[64,4096]{1,0:T(8,128)S(1)}, u32[]{:S(2)}, u32[]{:S(2)}) collective-permute-start(f32[64,4096]{1,0:T(8,128)S(1)} %get-tuple-element.373), channel_id=1, source_target_pairs={{0,2},{1,3},{2,0},{3,1},{4,6},{5,7},{6,4},{7,5},{8,10},{9,11},{10,... | collective-permute-start | bytes 3145736 | tf_op jit(solution)/shard_map/ppermute | solution.py:139
  375.8 32.9 %collective-permute-start.89 = (f32[32,4096]{1,0:T(8,128)S(1)}, f32[32,4096]{1,0:T(8,128)S(1)}, u32[]{:S(2)}, u32[]{:S(2)}) collective-permute-start(f32[32,4096]{1,0:T(8,128)S(1)} %get-tuple-element.370), channel_id=1, source_target_pairs={{0,2},{1,3},{2,0},{3,1},{4,6},{5,7},{6,4},{7,5},{8,10},{9,11},{10,... | collective-permute-start | bytes 1572872 | tf_op jit(solution)/shard_map/ppermute | solution.py:139
  (82 other events, 585.3 us)
